TPU v7x, 1024 devices: a whole 4x8x16 slice. The times are simulated.
1024 devices in a mesh: bl: 16 (over z), row: 8 (over x, y_hi), col: 8 (over y_lo, core).
Axes of the slice: x: 4, y: 8 (y_hi: 2, y_lo: 4; y = y_hi * 4 + y_lo), z: 16, core: 2. Of those that a mesh axis runs over, the one named last changes fastest.
Arguments:
- visibilities: bfloat16 [32768, 2, 1024], P(('bl', 'row', 'col')), may hold values from -6 to 6
- offsets: bfloat16 [32768, 2, 64], P(('bl', 'row', 'col')), may hold values from -6 to 6
- frequencies: float32 [16], replicated, may hold values from 0.8 to 1.2
- taper_curve: float32 [32], replicated, may hold values from 0.2 to 1
- owner_index: int32 [32768, 1], P(('bl', 'row', 'col')), may hold values from 0 to 63; in each aligned block of 32 rows (0 to 31, 32 to 63, ...) at most 2 rows name the same one
- tile_index: int32 [32768], P(('bl', 'row', 'col')), may hold values from 0 to 255
Outputs:
- dirty_rows: float32 [8, 128, 2, 16384], P('row', ('bl', 'col'))
Inputs may be any that keep to these rules, and one draw needn't show every extreme that they name: `owner_index`: owner index is pencil row times 8 plus pencil column; among the 32 blocks of one device no owner is named more than 2 times, a bound that some block reaches.
All inputs are finite; a program needn't handle non-finite values.
Results may differ from a plain program's by a relative error of at most 0.0036.
Values may be sent and summed in bfloat16 or wider, within the bound.
A program may use at most 64 MiB of HBM per device.

v0:
```python
import math

import jax
import jax.numpy as jnp
from jax import lax
from jax.sharding import PartitionSpec as P

SUB = 32
SPLIT = 128
GC = 16384
GR = 1024


def dft_tables(length):
    indices = jnp.arange(length, dtype=jnp.int32)
    product = indices[:, None] * indices[None, :] % length
    angles = 2.0 * math.pi / length * product.astype(jnp.float32)
    return (jnp.cos(angles), jnp.sin(angles))


def make_subgrids(visibilities, offsets, frequencies, taper_curve):
    block_count = visibilities.shape[0]
    time_count = offsets.shape[2]
    chan_count = frequencies.shape[0]
    sub_size = taper_curve.shape[0]
    shifted = offsets.astype(jnp.float32)
    scaled_u = (shifted[:, 0, :, None] * frequencies[None, None, :]).reshape(
        block_count, time_count * chan_count
    )
    scaled_v = (shifted[:, 1, :, None] * frequencies[None, None, :]).reshape(
        block_count, time_count * chan_count
    )
    pixels = jnp.arange(sub_size, dtype=jnp.float32) - float(sub_size // 2)
    phase_rows = 2.0 * math.pi / sub_size * scaled_u[:, :, None] * pixels[None, None, :]
    phase_cols = 2.0 * math.pi / sub_size * scaled_v[:, :, None] * pixels[None, None, :]
    vis_real = visibilities[:, 0, :, None].astype(jnp.float32)
    vis_imag = visibilities[:, 1, :, None].astype(jnp.float32)
    cos_rows = jnp.cos(phase_rows)
    sin_rows = jnp.sin(phase_rows)
    left_side = jnp.concatenate(
        [vis_real * cos_rows - vis_imag * sin_rows, vis_real * sin_rows + vis_imag * cos_rows],
        axis=2,
    ).astype(jnp.bfloat16)
    right_side = jnp.concatenate([jnp.cos(phase_cols), jnp.sin(phase_cols)], axis=2).astype(
        jnp.bfloat16
    )
    product = jnp.einsum("nkl,nkm->nlm", left_side, right_side, preferred_element_type=jnp.float32)
    real_part = product[:, :sub_size, :sub_size] - product[:, sub_size:, sub_size:]
    imag_part = product[:, :sub_size, sub_size:] + product[:, sub_size:, :sub_size]
    weights = taper_curve[:, None] * taper_curve[None, :] / math.sqrt(time_count * chan_count)
    real_part = real_part * weights[None]
    imag_part = imag_part * weights[None]
    cos_table, sin_table = dft_tables(sub_size)
    highest = lax.Precision.HIGHEST
    first_real = jnp.einsum("pj,njm->npm", cos_table, real_part, precision=highest) + jnp.einsum(
        "pj,njm->npm", sin_table, imag_part, precision=highest
    )
    first_imag = jnp.einsum("pj,njm->npm", cos_table, imag_part, precision=highest) - jnp.einsum(
        "pj,njm->npm", sin_table, real_part, precision=highest
    )
    final_real = jnp.einsum("npm,qm->npq", first_real, cos_table, precision=highest) + jnp.einsum(
        "npm,qm->npq", first_imag, sin_table, precision=highest
    )
    final_imag = jnp.einsum("npm,qm->npq", first_imag, cos_table, precision=highest) - jnp.einsum(
        "npm,qm->npq", first_real, sin_table, precision=highest
    )
    stacked = jnp.stack([final_real, final_imag], axis=2) / float(sub_size)
    return stacked.reshape(block_count, sub_size * 2 * sub_size)


def column_transform(whole_rows):
    row_count = whole_rows.shape[0]
    highest = lax.Precision.HIGHEST
    cos_table, sin_table = dft_tables(SPLIT)
    blocks_real = whole_rows[:, 0, :].reshape(row_count, SPLIT, SPLIT)
    blocks_imag = whole_rows[:, 1, :].reshape(row_count, SPLIT, SPLIT)
    section_real = jnp.einsum(
        "na,rab->rnb", cos_table, blocks_real, precision=highest
    ) - jnp.einsum("na,rab->rnb", sin_table, blocks_imag, precision=highest)
    section_imag = jnp.einsum(
        "na,rab->rnb", cos_table, blocks_imag, precision=highest
    ) + jnp.einsum("na,rab->rnb", sin_table, blocks_real, precision=highest)
    indices = jnp.arange(SPLIT, dtype=jnp.int32)
    twist = (indices[:, None] * indices[None, :] % GC).astype(jnp.float32) * (2.0 * math.pi / GC)
    twist_real = jnp.cos(twist)
    twist_imag = jnp.sin(twist)
    rotated_real = section_real * twist_real[None] - section_imag * twist_imag[None]
    rotated_imag = section_real * twist_imag[None] + section_imag * twist_real[None]
    final_real = jnp.einsum("mb,rnb->rmn", cos_table, rotated_real, precision=highest) - jnp.einsum(
        "mb,rnb->rmn", sin_table, rotated_imag, precision=highest
    )
    final_imag = jnp.einsum("mb,rnb->rmn", cos_table, rotated_imag, precision=highest) + jnp.einsum(
        "mb,rnb->rmn", sin_table, rotated_real, precision=highest
    )
    stacked = jnp.stack(
        [final_real.reshape(row_count, GC), final_imag.reshape(row_count, GC)], axis=1
    )
    return stacked / float(SPLIT)


def on_device(visibilities, offsets, frequencies, taper_curve, owner_index, tile_index):
    blocks = visibilities.shape[0]
    owners = lax.axis_size(("row", "col"))
    capacity = max(2, 2 * blocks // owners)
    my_index = lax.axis_index(("row", "col"))
    tiles_down = GR // lax.axis_size("row") // SUB
    pencil_cols = GC // lax.axis_size("col")
    tiles_across = pencil_cols // SUB
    tiles_owned = tiles_down * tiles_across
    gathered_owner, gathered_tile = (
        lax.all_gather(owner_index, ("row", "col"), axis=0, tiled=True),
        lax.all_gather(tile_index, ("row", "col"), axis=0, tiled=True),
    )
    source_owner = gathered_owner.reshape(owners, blocks)
    source_tile = gathered_tile.reshape(owners, blocks)
    matches = (source_owner == my_index).astype(jnp.int32)
    slot_rank = jnp.cumsum(matches, axis=1) - 1
    sources = jnp.arange(owners, dtype=jnp.int32)[:, None]
    targets = jnp.where(matches > 0, sources * capacity + slot_rank, owners * capacity)
    slot_tiles = (
        jnp.full((owners * capacity,), tiles_owned, jnp.int32)
        .at[targets.reshape(-1)]
        .set(source_tile.reshape(-1), mode="drop")
    )
    local_owner = owner_index[:, 0]
    onehot = (local_owner[:, None] == jnp.arange(owners, dtype=jnp.int32)[None, :]).astype(
        jnp.int32
    )
    local_rank = jnp.sum(jnp.cumsum(onehot, axis=0) * onehot, axis=1) - 1
    send_slot = local_owner * capacity + local_rank
    subgrids = make_subgrids(visibilities, offsets, frequencies, taper_curve)
    packed = (
        jnp.zeros((owners * capacity, subgrids.shape[1]), jnp.float32).at[send_slot].set(subgrids)
    )
    received = lax.all_to_all(
        packed.reshape(owners, capacity, subgrids.shape[1]),
        ("row", "col"),
        split_axis=0,
        concat_axis=0,
        tiled=True,
    )
    arrived_rows = received.reshape(owners * capacity, -1)
    partial_tiles = jax.ops.segment_sum(arrived_rows, slot_tiles, num_segments=tiles_owned + 1)[
        :tiles_owned
    ]
    partial_grid = (
        partial_tiles.reshape(tiles_down, tiles_across, SUB, 2, SUB)
        .transpose(0, 2, 3, 1, 4)
        .reshape(tiles_down * SUB, 2, pencil_cols)
    )
    row_share = lax.psum_scatter(partial_grid, "bl", scatter_dimension=0, tiled=True)
    whole_rows = lax.all_to_all(row_share, "col", split_axis=0, concat_axis=2, tiled=True)
    result = column_transform(whole_rows)
    return result[None]


def solution(mesh):
    in_specs = (
        P(("bl", "row", "col"), None, None),
        P(("bl", "row", "col"), None, None),
        P(),
        P(),
        P(("bl", "row", "col"), None),
        P(("bl", "row", "col")),
    )
    out_specs = P("row", ("bl", "col"), None, None)
    return jax.shard_map(
        on_device, mesh=mesh, in_specs=in_specs, out_specs=out_specs, check_vma=False
    )
```

profile of v0, /device:TPU:1, one launch (start us, length us, event | category | flops | bytes accessed | tf_op | source)
XLA Modules:
  0.0 470.6 jit_solution(17690105547948623569)
XLA Ops:
  9.1 1.2 fusion.179
  10.8 31.0 %fusion.8 = (bf16[32,1024,32]{1,2,0:T(8,128)(2,1)S(1)}, bf16[32,1024,32]{1,2,0:T(8,128)(2,1)S(1)}, bf16[32,1024,32]{1,2,0:T(8,128)(2,1)S(1)}, bf16[32,1024,32]{1,2,0:T(8,128)(2,1)S(1)}) fusion(f32[32,1024]{1,0:T(8,128)S(1)} %get-tuple-element.19, f32[32]{0:T(128)S(1)} %iota_add_fusion, f32[32,1024]{1,0:T(8,128)S(1)} %get-tuple-element.23, ...), kind=kLoop, calls=%fused_computation.15 | loop fusion | flops 12582912 | bytes 8913024 | tf_op jit(solution)/shard_map/convert.3
  41.8 1.9 fusion.10
  43.8 1.2 fusion.34
  44.9 1.2 fusion.32
  46.5 1.2 fusion.19
  48.7 1.2 fusion.20
  51.9 1.0 fusion.18
  53.8 1.4 reshape.324
  55.2 1.0 scatter_custom_fusion.1
  56.2 1.6 reshape.301
  57.8 18.5 %all-to-all-start = ((f32[64,2,2048]{2,1,0:T(2,128)}), f32[64,2,2048]{2,1,0:T(2,128)S(1)}, u32[]{:S(2)}, u32[]{:S(2)}) async-start(f32[64,2,2048]{2,1,0:T(2,128)} %reshape.301), calls=%async_computation | async-start | bytes 2097152 | tf_op jit(solution)/shard_map/all_to_all | solution.py:135
  76.4 1.3 dynamic-slice
  78.7 257.2 %all-reduce.2 = (s32[2048]{0:T(1024)S(1)}, s32[2048]{0:T(1024)S(1)}) all-reduce(s32[2048]{0:T(1024)S(1)} %bitcast_dynamic-update-slice_fusion, s32[2048]{0:T(1024)S(1)} %dynamic-update-slice.1), channel_id=1, replica_groups=mesh['bl'=16,'row'=8,'col'=8] {'row','col'}, use_global_device_ids=true, to_apply=%add | all-reduce | flops 4096 | bytes 32768
  336.4 8.0 %scatter_custom_fusion = s32[128]{0:T(128)S(1)} fusion(s32[2048]{0:T(1024)S(1)} %bitcast.114, s32[2048]{0:T(1024)S(1)} %get-tuple-element.6, s32[]{:T(128)} %constant.74.clone.1), kind=kCustom, calls=%fused_computation.125 | custom fusion | bytes 516 | tf_op jit(solution)/shard_map/scatter | solution.py:123
  345.2 2.7 scatter_custom_fusion.2
  347.8 1.5 slice.50
  349.3 1.9 copy.87
  351.3 3.1 reshape.303
  354.3 7.6 %copy.88 = f32[4,32,2,64,32]{4,3,1,0,2:T(8,128)} copy(f32[4,32,2,64,32]{3,0,4,2,1:T(4,128)} %bitcast.102) | data formatting | bytes 4194304 | tf_op jit(solution)/shard_map/transpose | solution.py:148
  361.9 7.5 %reshape.304 = f32[128,2,2048]{2,0,1:T(8,128)} reshape(f32[4,32,2,64,32]{4,3,1,0,2:T(8,128)} %copy.88) | data formatting | bytes 4194304 | tf_op jit(solution)/shard_map/reshape | solution.py:149
  369.5 65.2 %reduce-scatter.2.cloned.1.call-done = f32[8,2,2048]{2,0,1:T(8,128)} async-done(((f32[128,2,2048]{2,0,1:T(8,128)}), f32[8,2,2048]{2,0,1:T(8,128)}) %reduce-scatter.2.cloned.1.call-update) | async-done | bytes 131088 | tf_op jit(solution)/shard_map/reduce_scatter | solution.py:151
  434.7 1.0 copy.89
  435.7 21.8 %all_to_all.23 = f32[8,2,2048]{2,1,0:T(2,128)S(1)} all-to-all(f32[8,2,2048]{2,1,0:T(2,128)S(1)} %copy.89), channel_id=1, replica_groups=mesh['bl'=16,'row'=8,'col'=8] {'col'}, dimensions={0} | all-to-all | bytes 262144 | tf_op jit(solution)/shard_map/all_to_all | solution.py:152
  (53 shorter events, 15.1 us)
Async XLA Ops:
  41.8 4.3 copy-start
  53.0 25.3 %copy-start.1 = (s32[32]{0:T(128)S(1)}, s32[32]{0:T(128)}, u32[]{:S(2)}) copy-start(s32[32]{0:T(128)} %param.11) | copy-start | bytes 388
  57.8 286.6 %all-to-all-start = ((f32[64,2,2048]{2,1,0:T(2,128)}), f32[64,2,2048]{2,1,0:T(2,128)S(1)}, u32[]{:S(2)}, u32[]{:S(2)}) async-start(f32[64,2,2048]{2,1,0:T(2,128)} %reshape.301), calls=%async_computation | async-start | bytes 2097152 | tf_op jit(solution)/shard_map/all_to_all | solution.py:135
  76.3 358.4 %reduce-scatter.2.cloned.1.call-start = ((), (), s32[]{:S(2)}) async-start(), calls=%async_computation.3 | async-start | bytes 2228224 | tf_op jit(solution)/shard_map/reduce_scatter | solution.py:151
Sparse Core Ops, SparseCore 0:
  369.6 65.0 reduce-scatter.1
where the time goes:
time: 471 us
  blocking collectives  279 us (59%)
  waiting for transfers between devices  65.2 us (14%)
  local copies, waits for them, and re-layouts  41.6 us (9%)
  other arithmetic  36.1 us (8%)
  starting transfers between devices  18.5 us (4%)
  matrix products  15.7 us (3%)
  between operations  14.3 us (3%)
    unnamed x1, blocking collectives  257 us
    reduce_scatter x1, waiting for transfers between devices, on_device(): lax.psum_scatter(partial_grid, 'bl', scatter_dimension=0, tiled=True)  65.2 us
    another operation x1, other arithmetic  31 us
    all_to_all x1, blocking collectives, on_device(): lax.all_to_all(row_share, 'col', split_axis=0, concat_axis=2, tiled=True)  21.8 us
    all_to_all x1, starting transfers between devices, on_device(): lax.all_to_all(packed.reshape(owners, capacity, subgrids.shape[1]), ('row...  18.5 us
  transfers between devices with their start and end apart: 2, of which 1 were waited for; matrix products, arithmetic and copies ran while one was open for 2% of the time, Pallas kernels for 0%

commit v1 on v0

v1 whole, which is shorter than its diff:
```python
import math

import jax
import jax.numpy as jnp
import numpy as np
from jax import lax
from jax.experimental import pallas as pl
from jax.experimental.pallas import tpu as pltpu
from jax.sharding import PartitionSpec as P

MESH = pl.DeviceIdType.MESH
SUB = 32
GC = 16384
TILES = GC // SUB
GROUP = 64
F32 = jnp.float32
BF16 = jnp.bfloat16


def split_np(table):
    high = table.astype(BF16)
    low = (table - high.astype(np.float64)).astype(BF16)
    return np.stack([high, low])


def make_tables():
    index = np.arange(SUB)
    angle = 2.0 * np.pi * (index[:, None] * index[None, :] % SUB) / SUB
    cos, sin = np.cos(angle), np.sin(angle)
    rows = np.zeros((2, 4, SUB, 4, 2, SUB))
    for b in range(4):
        rows[0, b, :, b, 0], rows[0, b, :, b, 1] = cos, sin
        rows[1, b, :, b, 0], rows[1, b, :, b, 1] = -sin, cos
    rows = rows.reshape(256, 256)
    from_real = np.block([[cos, -sin], [sin, cos]])
    from_imag = np.block([[sin, cos], [-cos, sin]])
    cols = np.zeros((2, 2, 256, 128))
    for half in range(2):
        cols[half, 0, :, half * 64 : half * 64 + 64] = np.tile(from_real, (4, 1))
        cols[half, 1, :, half * 64 : half * 64 + 64] = np.tile(from_imag, (4, 1))
    cols = cols.reshape(4, 256, 128)
    wide = np.arange(TILES)
    wide_angle = 2.0 * np.pi * (wide[:, None] * wide[None, :] % TILES) / TILES
    wide_table = np.concatenate([np.cos(wide_angle), np.sin(wide_angle)], axis=1)
    twist_angle = 2.0 * np.pi * (index[:, None] * wide[None, :]) / GC
    twist = (np.stack([np.cos(twist_angle), np.sin(twist_angle)]) / 128.0).astype(np.float32)
    last = np.block([[cos, -sin], [sin, cos]])
    return split_np(rows), split_np(cols), split_np(wide_table), twist, split_np(last)


def dot(a, b):
    return lax.dot_general(a, b, (((1,), (0,)), ((), ())), preferred_element_type=F32)


def dot_t(a, b):
    return lax.dot_general(a, b, (((1,), (1,)), ((), ())), preferred_element_type=F32)


def split(x):
    high = x.astype(BF16)
    return high, (x - high.astype(F32)).astype(BF16)


def cmul(ar, ai, br, bi):
    return ar * br - ai * bi, ar * bi + ai * br


def phasors(off_ref, freq_ref, z_ref):
    spread = (
        lax.broadcasted_iota(jnp.int32, (64, 1024), 1) // 16
        == lax.broadcasted_iota(jnp.int32, (64, 1024), 0)
    ).astype(F32).astype(BF16)
    scaled = dot(off_ref[...], spread) * freq_ref[...]
    theta = scaled * (2.0 * math.pi / SUB)
    square = theta * theta
    cos, sin = jnp.full_like(square, 1.0 / math.factorial(14)), jnp.full_like(
        square, 1.0 / math.factorial(15)
    )
    for order in range(6, -1, -1):
        sign = 1.0 if order % 2 == 0 else -1.0
        if order == 6:
            cos, sin = -cos, -sin
        cos = cos * square + sign / math.factorial(2 * order)
        sin = sin * square + sign / math.factorial(2 * order + 1)
    real, imag = cos, sin * theta
    for e in range(5):
        z_ref[e, 0], z_ref[e, 1] = real, imag
        if e < 4:
            real, imag = real * real - imag * imag, 2.0 * real * imag


def powers(base_r, base_i, z8, z16):
    parts = [
        cmul(base_r, base_i, z16[0], -z16[1]),
        cmul(base_r, base_i, z8[0], -z8[1]),
        (base_r, base_i),
        cmul(base_r, base_i, z8[0], z8[1]),
    ]
    real = jnp.concatenate([part[0] for part in parts], axis=0)
    imag = jnp.concatenate([part[1] for part in parts], axis=0)
    return jnp.concatenate([real, imag], axis=0).astype(BF16)


def block_sides(block, slot, vis_ref, z_ref, left_ref, right_ref):
    chunk = 256
    sub = lax.broadcasted_iota(jnp.int32, (8, chunk), 0)
    rows = pl.ds(pl.multiple_of(slot * 64, 64), 64)
    for start in range(0, 1024, chunk):
        lanes = pl.ds(start, chunk)
        for side in range(2):
            row = pl.ds(2 * block + side, 1)

            def z(e):
                return [jnp.broadcast_to(z_ref[e, part, row, lanes], (8, chunk)) for part in (0, 1)]

            base_r, base_i = jnp.where(sub & 1, z(0)[0], 1.0), jnp.where(sub & 1, z(0)[1], 0.0)
            for e in (1, 2):
                bit = (sub & (1 << e)) != 0
                zr, zi = z(e)
                base_r, base_i = cmul(
                    base_r, base_i, jnp.where(bit, zr, 1.0), jnp.where(bit, zi, 0.0)
                )
            if side == 0:
                vis = vis_ref[block, :, lanes].astype(F32)
                base_r, base_i = cmul(base_r, base_i, vis[0:1], vis[1:2])
            target = left_ref if side == 0 else right_ref
            target[rows, lanes] = powers(base_r, base_i, z(3), z(4))


def subgrids(vis_ref, w_ref, rows_ref, cols_ref, z_ref, left_ref, right_ref, sub_ref):
    def pair(gp, _):
        def one(slot, _):
            block_sides(gp * 8 + slot, slot, vis_ref, z_ref, left_ref, right_ref)
            return 0

        lax.fori_loop(0, 8, one, 0)
        total = jnp.zeros((128, 128), F32)
        for half in range(2):
            four = slice(half * 256, half * 256 + 256)
            image = dot_t(left_ref[four], right_ref[four]) * w_ref[...]
            high, low = split(image)
            first = dot(rows_ref[0], high) + dot(rows_ref[0], low) + dot(rows_ref[1], high)
            high, low = split(first)
            for part in range(2):
                use = slice(part * 128, part * 128 + 128)
                k = 2 * half + part
                total += dot(high[use], cols_ref[0, k]) + dot(low[use], cols_ref[0, k])
                total += dot(high[use], cols_ref[1, k])
        for b in range(4):
            sub_ref[pl.ds(gp * 4 + b, SUB, stride=16), :] = total[b * 32 : b * 32 + 32]
        return 0

    lax.fori_loop(0, 4, pair, 0)


def column_transform(grid, wide_ref, twist_ref, last_ref):
    high, low = split(grid)
    wide = dot(high, wide_ref[0]) + dot(low, wide_ref[0]) + dot(high, wide_ref[1])
    real = wide[:SUB, :TILES] - wide[SUB:, TILES:]
    imag = wide[SUB:, :TILES] + wide[:SUB, TILES:]
    real, imag = cmul(real, imag, twist_ref[0], twist_ref[1])
    high, low = split(jnp.concatenate([real, imag], axis=0))
    return dot(last_ref[0], high) + dot(last_ref[0], low) + dot(last_ref[1], high)


def kernel(
    vis_ref,
    off_ref,
    freq_ref,
    w_ref,
    place_ref,
    rows_ref,
    cols_ref,
    wide_hbm,
    twist_ref,
    last_ref,
    out_ref,
    z_ref,
    left_ref,
    right_ref,
    sub_ref,
    send_ref,
    got_ref,
    places_ref,
    data_ref,
    onehot_ref,
    masked_ref,
    own_ref,
    xsend_ref,
    xgot_ref,
    zsend_ref,
    zgot_ref,
    wide_ref,
    local_sem,
    psend_sem,
    pgot_sem,
    ssend_sem,
    sgot_sem,
    xsend_sem,
    xgot_sem,
    zsend_sem,
    zgot_sem,
):
    bl, row, col = lax.axis_index("bl"), lax.axis_index("row"), lax.axis_index("col")
    high_z, low_z = bl // 4, bl % 4
    x, y_hi = row // 2, row % 2
    me = y_hi * 32 + low_z * 8 + col

    def member(slot):
        return (high_z * 4 + slot % 32 // 8, x * 2 + slot // 32, slot % 8)

    def along_x(step):
        return (bl, (x + step) % 4 * 2 + y_hi, col)

    def along_z(step):
        return ((high_z + step) % 4 * 4 + low_z, row, col)

    barrier = pltpu.get_barrier_semaphore()

    def greet(step, _):
        pl.semaphore_signal(
            barrier, inc=1, device_id=member((me + step) % GROUP), device_id_type=MESH
        )
        return 0

    lax.fori_loop(1, GROUP, greet, 0)
    for step in range(1, 4):
        pl.semaphore_signal(barrier, inc=1, device_id=along_x(step), device_id_type=MESH)
        pl.semaphore_signal(barrier, inc=1, device_id=along_z(step), device_id_type=MESH)
    wide_copy = pltpu.make_async_copy(wide_hbm, wide_ref, local_sem)
    wide_copy.start()

    phasors(off_ref, freq_ref, z_ref)
    pl.semaphore_wait(barrier, GROUP - 1 + 6)

    def place_copy(step):
        return pltpu.make_async_remote_copy(
            src_ref=place_ref,
            dst_ref=places_ref.at[me],
            send_sem=psend_sem.at[step],
            recv_sem=pgot_sem.at[me],
            device_id=member((me + step) % GROUP),
            device_id_type=MESH,
        )

    def sub_copy(step):
        slot = (me + step) % GROUP
        return pltpu.make_async_remote_copy(
            src_ref=send_ref.at[slot % 32],
            dst_ref=got_ref.at[me],
            send_sem=ssend_sem.at[step],
            recv_sem=sgot_sem.at[me],
            device_id=member(slot),
            device_id_type=MESH,
        )

    def start(copy):
        def body(step, _):
            copy(step).start()
            return 0

        lax.fori_loop(1, GROUP, body, 0)

    def finish_sends(copy):
        def body(step, _):
            copy(step).wait_send()
            return 0

        lax.fori_loop(1, GROUP, body, 0)

    def finish_gets(buffer, sem):
        def body(step, _):
            slot = (me + step) % GROUP
            pltpu.make_async_copy(buffer.at[slot], buffer.at[slot], sem.at[slot]).wait()
            return 0

        lax.fori_loop(1, GROUP, body, 0)

    start(place_copy)
    places_ref[me] = place_ref[...]
    subgrids(vis_ref, w_ref, rows_ref, cols_ref, z_ref, left_ref, right_ref, sub_ref)
    send_ref[...] = sub_ref[...].astype(BF16).reshape(SUB, 16, 128)
    start(sub_copy)
    got_ref[me] = send_ref[me % 32]

    finish_gets(places_ref, pgot_sem)
    diagonal = (
        lax.broadcasted_iota(jnp.int32, (8, 128), 1) // 16
        == lax.broadcasted_iota(jnp.int32, (8, 128), 0)
    )
    tile_rows = []
    for k in range(16):
        pieces = places_ref[pl.ds(k // 2 * 8, 8), k % 2, :]
        place = jnp.sum(jnp.where(diagonal, pieces, 0), axis=0, keepdims=True)
        tile_rows.append(place // TILES)
        onehot_ref[:, pl.ds(k * 128, 128)] = (
            (lax.broadcasted_iota(jnp.int32, (TILES, 128), 0) == place % TILES)
            .astype(F32)
            .astype(BF16)
        )
    tile_row = jnp.concatenate(tile_rows, axis=1)

    finish_gets(got_ref, sgot_sem)
    for k in range(8):
        turned = got_ref[pl.ds(k * 8, 8)].reshape(128, 128).astype(F32).T.astype(BF16)
        data_ref[:, pl.ds(k * 256, 128)] = turned[:64]
        data_ref[:, pl.ds(k * 256 + 128, 128)] = turned[64:]

    def x_copy(turn, step):
        return pltpu.make_async_remote_copy(
            src_ref=xsend_ref.at[turn, step - 1],
            dst_ref=xgot_ref.at[turn, step - 1],
            send_sem=xsend_sem.at[turn, step - 1],
            recv_sem=xgot_sem.at[turn, step - 1],
            device_id=along_x(step),
            device_id_type=MESH,
        )

    def z_copy(turn):
        return pltpu.make_async_remote_copy(
            src_ref=zsend_ref.at[turn],
            dst_ref=zgot_ref.at[turn],
            send_sem=zsend_sem.at[turn],
            recv_sem=zgot_sem.at[turn],
            device_id=along_z((2, 1, 3)[turn]),
            device_id_type=MESH,
        )

    for turn in range(4):
        td = (high_z + (2, 1, 3, 0)[turn]) % 4
        for step in range(4):
            wanted = ((x + step) % 4 * 2 + y_hi) * 4 + td
            masked_ref[pl.ds(step * 64, 64), :] = jnp.where(
                tile_row == wanted, data_ref[...].astype(F32), 0.0
            ).astype(BF16)
        placed = dot_t(masked_ref[...], onehot_ref[...])
        own_ref[turn] = placed[:64]
        for step in (2, 1, 3):
            xsend_ref[turn, step - 1] = placed[step * 64 : step * 64 + 64].astype(BF16)
            x_copy(turn, step).start()

    for turn in range(4):
        total = own_ref[turn]
        for step in range(1, 4):
            x_copy(turn, step).wait_recv()
            total += xgot_ref[turn, step - 1].astype(F32)
        if turn < 3:
            zsend_ref[turn] = total.astype(BF16)
            z_copy(turn).start()
        else:
            own_ref[turn] = total

    finish_sends(place_copy)
    finish_sends(sub_copy)
    for turn in range(4):
        for step in range(1, 4):
            x_copy(turn, step).wait_send()
    wide_copy.wait()
    grid = own_ref[3]
    for turn in range(3):
        z_copy(turn).wait_recv()
        grid += zgot_ref[turn].astype(F32)
    out_ref[...] = column_transform(grid, wide_ref, twist_ref, last_ref)
    for turn in range(3):
        z_copy(turn).wait_send()


def on_device(visibilities, offsets, frequencies, taper_curve, owner_index, tile_index):
    rows, cols, wide, twist, last = make_tables()
    mask = np.kron(np.eye(4), np.ones((64, 64))).astype(np.float32) / 1024.0
    taper = jnp.tile(taper_curve, 8)
    weights = taper[:, None] * taper[None, :] * mask
    owner = owner_index[:, 0]
    place = (owner // 8 * 4 + tile_index // 64) * TILES + owner % 8 * 64 + tile_index % 64
    place = place.reshape(4, 2, 4).transpose(1, 0, 2).reshape(2, 1, 16)
    place = jnp.broadcast_to(place, (2, 8, 16)).reshape(2, 128)
    vmem = pl.BlockSpec(memory_space=pltpu.VMEM)
    result = pl.pallas_call(
        kernel,
        out_shape=jax.ShapeDtypeStruct((64, TILES), F32),
        in_specs=[vmem] * 7 + [pl.BlockSpec(memory_space=pl.ANY)] + [vmem] * 2,
        out_specs=vmem,
        scratch_shapes=[
            pltpu.VMEM((5, 2, 64, 1024), F32),
            pltpu.VMEM((512, 1024), BF16),
            pltpu.VMEM((512, 1024), BF16),
            pltpu.VMEM((512, 128), F32),
            pltpu.VMEM((SUB, 16, 128), BF16),
            pltpu.VMEM((GROUP, 16, 128), BF16),
            pltpu.VMEM((GROUP, 2, 128), jnp.int32),
            pltpu.VMEM((64, 2048), BF16),
            pltpu.VMEM((TILES, 2048), BF16),
            pltpu.VMEM((256, 2048), BF16),
            pltpu.VMEM((4, 64, TILES), F32),
            pltpu.VMEM((4, 3, 64, TILES), BF16),
            pltpu.VMEM((4, 3, 64, TILES), BF16),
            pltpu.VMEM((3, 64, TILES), BF16),
            pltpu.VMEM((3, 64, TILES), BF16),
            pltpu.VMEM((2, TILES, 2 * TILES), BF16),
            pltpu.SemaphoreType.DMA,
            pltpu.SemaphoreType.DMA((GROUP,)),
            pltpu.SemaphoreType.DMA((GROUP,)),
            pltpu.SemaphoreType.DMA((GROUP,)),
            pltpu.SemaphoreType.DMA((GROUP,)),
            pltpu.SemaphoreType.DMA((4, 3)),
            pltpu.SemaphoreType.DMA((4, 3)),
            pltpu.SemaphoreType.DMA((3,)),
            pltpu.SemaphoreType.DMA((3,)),
        ],
        compiler_params=pltpu.CompilerParams(
            collective_id=0, has_side_effects=True, vmem_limit_bytes=40 * 1024 * 1024
        ),
    )(
        visibilities,
        offsets.reshape(64, 64),
        jnp.tile(frequencies, 64).reshape(1, 1024),
        weights,
        place,
        jnp.asarray(rows),
        jnp.asarray(cols),
        jnp.asarray(wide),
        jnp.asarray(twist),
        jnp.asarray(last),
    )
    return result.reshape(1, 1, 2, GC)


def solution(mesh):
    in_specs = (
        P(("bl", "row", "col"), None, None),
        P(("bl", "row", "col"), None, None),
        P(),
        P(),
        P(("bl", "row", "col"), None),
        P(("bl", "row", "col")),
    )
    out_specs = P("row", ("bl", "col"), None, None)
    return jax.shard_map(
        on_device, mesh=mesh, in_specs=in_specs, out_specs=out_specs, check_vma=False
    )
```

time: 471 us -> 83 us (0.18)
  blocking collectives: 279 us -> 0 us
  Pallas kernels: 0 us -> 71.2 us
  waiting for transfers between devices: 65.2 us -> 0 us
  other arithmetic: 36.1 us -> 1.74 us
  local copies, waits for them, and re-layouts: 41.6 us -> 9.37 us
  starting transfers between devices: 18.5 us -> 0 us
  matrix products: 15.7 us -> 0 us
  between operations: 14.3 us -> 0.04 us
    unnamed x1 -> x0, blocking collectives: 257 us -> none
    pallas_call x0 -> x1, Pallas kernels: none -> 71.2 us  [on_device(): pl.pallas_call(kernel, out_shape=jax.ShapeDtypeStruct((64, TILES), F32),...]
    reduce_scatter x1 -> x0, waiting for transfers between devices: 65.2 us -> none  [on_device(): lax.psum_scatter(partial_grid, 'bl', scatter_dimension=0, tiled=True)]
    another operation x3 -> x0, other arithmetic: 31.3 us -> none
    all_to_all x1 -> x0, blocking collectives: 21.8 us -> none  [on_device(): lax.all_to_all(row_share, 'col', split_axis=0, concat_axis=2, tiled=True)]
    all_to_all x1 -> x0, starting transfers between devices: 18.5 us -> none  [on_device(): lax.all_to_all(packed.reshape(owners, capacity, subgrids.shape[1]), ('row...]
    dot_general x17 -> x0, matrix products: 15.7 us -> none  [the longest x1 1.91 us: make_subgrids(): jnp.einsum('nkl,nkm->nlm', left_side, right_side, preferred_element_type=...]
    reshape x4 -> x3, local copies, waits for them, and re-layouts: 12.9 us -> 0.93 us  [the longest x1 0.76 us: on_device(): return result.reshape(1, 1, 2, GC)]
  transfers between devices with their start and end apart: 2 -> 0, of which waited for: 1 -> 0; matrix products, arithmetic and copies ran while one was open for 2% -> 0% of each run, Pallas kernels for 0% -> 0%
where the time goes in v1:
time: 83 us; the launch traced here: 82.4 us
  Pallas kernels  71.2 us (86%)
  local copies, waits for them, and re-layouts  9.37 us (11%)
  other arithmetic  1.74 us (2%)
    pallas_call x1, Pallas kernels, on_device(): pl.pallas_call(kernel, out_shape=jax.ShapeDtypeStruct((64, TILES), F32),...  71.2 us
    unnamed x14, local copies, waits for them, and re-layouts  6.86 us

profile of v1, /device:TPU:1, one launch (start us, length us, event | category | flops | bytes accessed | tf_op | source)
XLA Modules:
  0.0 82.4 jit_solution(4136210677595201873)
XLA Ops:
  0.0 0.7 fusion
  0.7 0.1 reshape.19
  0.8 0.1 broadcast_in_dim.7
  0.9 0.7 tile.5
  1.5 0.1 mul.34
  1.6 0.1 reshape.20.place_ref
  1.7 0.7 tile.4
  2.4 0.1 reshape_tile.3.freq_ref
  2.4 1.1 %multiply_multiply_fusion.w_ref = f32[256,256]{1,0:T(8,128)S(1)} fusion(f32[256,256]{1,0:T(8,128)} %constant.65.clone, f32[256]{0:T(256)S(1)} %mul.34), kind=kLoop, calls=%fused_computation | loop fusion | flops 131072 | bytes 525312 | tf_op jit(solution)/shard_map/mul | solution.py:372
  3.5 0.0 copy-start
  3.5 1.6 %copy-done = bf16[2,512,1024]{2,1,0:T(8,128)(2,1)S(1)} copy-done((bf16[2,512,1024]{2,1,0:T(8,128)(2,1)S(1)}, bf16[2,512,1024]{2,1,0:T(8,128)(2,1)}, u32[]{:S(2)}) %copy-start) | copy-done | bytes 2097176
  5.1 0.0 copy-start.1
  5.1 1.0 %copy-done.1 = bf16[2,4,256,128]{3,2,1,0:T(8,128)(2,1)S(1)} copy-done((bf16[2,4,256,128]{3,2,1,0:T(8,128)(2,1)S(1)}, bf16[2,4,256,128]{3,2,1,0:T(8,128)(2,1)}, u32[]{:S(2)}) %copy-start.1) | copy-done | bytes 524312
  6.1 0.0 copy-start.2
  6.1 0.9 %copy-done.2 = bf16[2,256,256]{2,1,0:T(8,128)(2,1)S(1)} copy-done((bf16[2,256,256]{2,1,0:T(8,128)(2,1)S(1)}, bf16[2,256,256]{2,1,0:T(8,128)(2,1)}, u32[]{:S(2)}) %copy-start.2) | copy-done | bytes 262168
  7.1 0.0 copy-start.3
  7.1 0.9 %copy-done.3 = bf16[32,2,1024]{2,1,0:T(2,128)(2,1)S(1)} copy-done((bf16[32,2,1024]{2,1,0:T(2,128)(2,1)S(1)}, bf16[32,2,1024]{2,1,0:T(2,128)(2,1)}, u32[]{:S(2)}) %copy-start.3) | copy-done | bytes 131096
  8.0 0.0 copy-start.4
  8.0 0.9 %copy-done.4 = f32[2,32,512]{2,1,0:T(8,128)S(1)} copy-done((f32[2,32,512]{2,1,0:T(8,128)S(1)}, f32[2,32,512]{2,1,0:T(8,128)}, u32[]{:S(2)}) %copy-start.4) | copy-done | bytes 131096
  8.9 0.0 copy-start.5
  8.9 0.8 copy-done.5
  9.7 0.7 copy-done.6
  10.4 71.2 %shard_map.118 = f32[64,512]{1,0:T(8,128)S(1)} custom-call(bf16[32,2,1024]{2,1,0:T(2,128)(2,1)S(1)} %copy-done.3, bf16[64,64]{1,0:T(8,128)(2,1)S(1)} %bitcast.15, f32[1,1024]{1,0:T(1,128)S(1)} %reshape_tile.3.freq_ref, f32[256,256]{1,0:T(8,128)S(1)} %multiply_multiply_fusion.w_ref, s32[2,128]{1,0:T(2,128)S(1)} %reshape.20.place_ref, ...), custom_call_target="tpu_custom_call" | custom-call | tf_op jit(solution)/shard_map/pallas_call | solution.py:378
  81.6 0.8 reshape.21
  (3 shorter events, 0.0 us)
Async XLA Ops:
  3.5 1.6 %copy-start = (bf16[2,512,1024]{2,1,0:T(8,128)(2,1)S(1)}, bf16[2,512,1024]{2,1,0:T(8,128)(2,1)}, u32[]{:S(2)}) copy-start(bf16[2,512,1024]{2,1,0:T(8,128)(2,1)} %constant.68.clone.wide_hbm) | copy-start | bytes 6291460
  5.1 1.0 %copy-start.1 = (bf16[2,4,256,128]{3,2,1,0:T(8,128)(2,1)S(1)}, bf16[2,4,256,128]{3,2,1,0:T(8,128)(2,1)}, u32[]{:S(2)}) copy-start(bf16[2,4,256,128]{3,2,1,0:T(8,128)(2,1)} %constant.67.clone.cols_ref) | copy-start | bytes 1572868
  6.1 0.9 %copy-start.2 = (bf16[2,256,256]{2,1,0:T(8,128)(2,1)S(1)}, bf16[2,256,256]{2,1,0:T(8,128)(2,1)}, u32[]{:S(2)}) copy-start(bf16[2,256,256]{2,1,0:T(8,128)(2,1)} %constant.66.clone.rows_ref) | copy-start | bytes 786436
  7.1 0.9 %copy-start.3 = (bf16[32,2,1024]{2,1,0:T(2,128)(2,1)S(1)}, bf16[32,2,1024]{2,1,0:T(2,128)(2,1)}, u32[]{:S(2)}) copy-start(bf16[32,2,1024]{2,1,0:T(2,128)(2,1)} %vis_ref.1) | copy-start | bytes 393220
  8.0 0.9 %copy-start.4 = (f32[2,32,512]{2,1,0:T(8,128)S(1)}, f32[2,32,512]{2,1,0:T(8,128)}, u32[]{:S(2)}) copy-start(f32[2,32,512]{2,1,0:T(8,128)} %constant.69.clone.twist_ref) | copy-start | bytes 393220
  8.9 0.8 copy-start.5
  9.7 0.7 copy-start.6

commit v2 on v1

v2 whole, which is shorter than its diff:
```python
import math

import jax
import jax.numpy as jnp
import numpy as np
from jax import lax
from jax.experimental import pallas as pl
from jax.experimental.pallas import tpu as pltpu
from jax.sharding import PartitionSpec as P

MESH = pl.DeviceIdType.MESH
SUB = 32
GC = 16384
TILES = GC // SUB
GROUP = 64
F32 = jnp.float32
BF16 = jnp.bfloat16


def split_np(table):
    high = table.astype(BF16)
    low = (table - high.astype(np.float64)).astype(BF16)
    return np.stack([high, low])


def by_lanes(table):
    rows, lanes = table.shape[-2:]
    pieces = table.reshape(table.shape[:-1] + (lanes // 128, 128))
    return np.ascontiguousarray(np.moveaxis(pieces, -2, -3))


def joined(ref, *index):
    return jnp.concatenate([ref[(*index, k)] for k in range(ref.shape[-3])], axis=1)


def make_tables():
    index = np.arange(SUB)
    angle = 2.0 * np.pi * (index[:, None] * index[None, :] % SUB) / SUB
    cos, sin = np.cos(angle), np.sin(angle)
    order = pixel_order()
    cos_in, sin_in = cos[:, order], sin[:, order]
    rows = np.zeros((2, 4, SUB, 4, 2, SUB))
    for b in range(4):
        rows[0, b, :, b, 0], rows[0, b, :, b, 1] = cos_in, sin_in
        rows[1, b, :, b, 0], rows[1, b, :, b, 1] = sin_in, -cos_in
    rows = split_np(rows.reshape(2, 128, 256))
    cos_in, sin_in = cos[order], sin[order]
    cols = np.block([[cos_in, -sin_in, -sin_in, -cos_in], [sin_in, cos_in, cos_in, -sin_in]])
    cols = split_np(np.tile(cols, (2, 1)))
    cols = np.concatenate([cols[0], cols[0], cols[1]])
    wide = np.arange(TILES)
    wide_angle = 2.0 * np.pi * (wide[:, None] * wide[None, :] % TILES) / TILES
    wide_table = np.concatenate([np.cos(wide_angle), np.sin(wide_angle)], axis=1)
    twist_angle = 2.0 * np.pi * (index[:, None] * wide[None, :]) / GC
    twist = (np.stack([np.cos(twist_angle), np.sin(twist_angle)]) / 128.0).astype(np.float32)
    last = np.block([[cos, -sin], [sin, cos]])
    return (
        by_lanes(rows),
        cols,
        by_lanes(split_np(wide_table)),
        twist,
        split_np(last),
    )


def dot(a, b):
    return lax.dot_general(a, b, (((1,), (0,)), ((), ())), preferred_element_type=F32)


def dot_t(a, b):
    return lax.dot_general(a, b, (((1,), (1,)), ((), ())), preferred_element_type=F32)


def split(x):
    high = x.astype(BF16)
    return high, (x - high.astype(F32)).astype(BF16)


def cmul(ar, ai, br, bi):
    return ar * br - ai * bi, ar * bi + ai * br


def three(x, rows):
    high = x.astype(BF16).astype(F32)
    middle = (x - high).astype(BF16).astype(F32)
    low = x - high - middle
    place = lax.broadcasted_iota(jnp.int32, (rows, x.shape[1]), 0)
    parts = jnp.where(place == 0, high, jnp.where(place == 1, middle, jnp.where(place == 2, low, 0.0)))
    return parts.astype(BF16)


def matches(shape, left, right):
    row, lane = lax.broadcasted_iota(jnp.int32, shape, 0), lax.broadcasted_iota(jnp.int32, shape, 1)
    return (left(row) == right(lane)).astype(F32).astype(BF16)


def pixel(k):
    slot = k % SUB
    return 16 + jnp.where(slot < 16, slot, jnp.where(slot == 16, -16, 16 - slot))


def weights(taper_ref, w_ref):
    parts = three(taper_ref[...], 16)
    along = dot(parts, matches((SUB, 128), lambda i: i, pixel))
    down = dot_t(matches((64, SUB), pixel, lambda k: k), parts)
    along, down = jnp.sum(along, axis=0, keepdims=True), jnp.sum(down, axis=1, keepdims=True)
    lane = lax.broadcasted_iota(jnp.int32, (64, 128), 1) // 64
    for half in range(2):
        w_ref[half] = jnp.where(lane == half, down * along * (1.0 / 1024.0), 0.0)


def places(owner_ref, tile_ref, place_ref):
    row = lax.broadcasted_iota(jnp.int32, (16, SUB), 0)
    parts = jnp.where(row == 0, owner_ref[...], jnp.where(row == 1, tile_ref[...], 0))
    order = matches(
        (SUB, 256), lambda i: i, lambda k: k % 16 // 4 * 8 + k // 128 * 4 + k % 4
    )
    both = dot(parts.astype(F32).astype(BF16), order).astype(jnp.int32)
    owner, tile = both[0:1], both[1:2]
    place_ref[...] = (owner // 8 * 4 + tile // 64) * TILES + owner % 8 * 64 + tile % 64


def phasors(off_ref, freq_ref, base_ref, far_ref):
    spread = matches((64, 1024), lambda i: i, lambda k: k // 16)
    repeat = matches((16, 1024), lambda i: i, lambda k: k % 16)
    freq = jnp.sum(dot(three(freq_ref[...], 16), repeat), axis=0, keepdims=True)
    scaled = dot(off_ref[...], spread) * freq
    theta = scaled * (2.0 * math.pi / SUB)
    square = theta * theta
    cos = jnp.full_like(square, -1.0 / math.factorial(14))
    sin = jnp.full_like(square, -1.0 / math.factorial(15))
    for order in range(6, -1, -1):
        sign = 1.0 if order % 2 == 0 else -1.0
        cos = cos * square + sign / math.factorial(2 * order)
        sin = sin * square + sign / math.factorial(2 * order + 1)
    z = [(jnp.ones_like(cos), jnp.zeros_like(cos)), (cos, sin * theta)]
    for p in range(2, 8):
        z.append(cmul(*z[p // 2], *z[p - p // 2]))
    for p in range(8):
        for part in range(2):
            for k in range(8):
                base_ref[part, k, pl.ds(p * 65, 64)] = z[p][part][:, k * 128 : k * 128 + 128]
    z8 = cmul(*z[4], *z[4])
    for e, value in enumerate((z8, cmul(*z8, *z8))):
        for part in range(2):
            far_ref[e, part] = value[part]


def pixel_order():
    slot = np.arange(SUB)
    return 16 + np.where(slot < 16, slot, np.where(slot == 16, -16, 16 - slot))


def block_sides(block, slot, vis_ref, base_ref, far_ref, left_ref, right_ref):
    chunk = 256
    first = lax.broadcasted_iota(jnp.int32, (8, chunk), 0) == 0
    for start in range(0, 1024, chunk):
        lanes = pl.ds(start, chunk)
        for side, target in enumerate((left_ref, right_ref)):
            row = 2 * block + side
            low = [
                jnp.concatenate(
                    [
                        base_ref[part, start // 128 + k, pl.ds(row, 8, stride=65), :]
                        for k in range(chunk // 128)
                    ],
                    axis=1,
                )
                for part in (0, 1)
            ]
            far = [
                [jnp.broadcast_to(far_ref[e, part, pl.ds(row, 1), lanes], (8, chunk)) for part in (0, 1)]
                for e in (0, 1)
            ]
            near = (low, cmul(*low, *far[0]))
            if side == 0:
                vis = vis_ref[block, :, lanes].astype(F32)
                vr, vi = (jnp.broadcast_to(vis[k : k + 1], (8, chunk)) for k in (0, 1))
                products = [(vr * c, vi * s, vr * s, vi * c) for c, s in near]
                plus = [(a - b, d + e) for a, b, d, e in products]
                minus = [(a + b, e - d) for a, b, d, e in products]
                last = cmul(vr, vi, far[1][0], -far[1][1])
            else:
                plus, minus = near, [(c, -s) for c, s in near]
                last = (far[1][0], -far[1][1])
            minus[0] = tuple(jnp.where(first, x, y) for x, y in zip(last, minus[0]))
            for part in range(2):
                for k, pieces in enumerate((plus, minus)):
                    rows = pl.ds(slot * 64 + part * 32 + k * 16, 16)
                    target[rows, lanes] = jnp.concatenate(
                        [piece[part] for piece in pieces], axis=0
                    ).astype(BF16)


def subgrids(vis_ref, w_ref, rows_ref, cols_ref, base_ref, far_ref, side_refs, image_ref, sub_ref):
    def sides(four, which):
        for b in range(4):
            block_sides(four * 4 + b, b, vis_ref, base_ref, far_ref, *side_refs[which])

    def image(four, which):
        left_ref, right_ref = side_refs[which]
        product = dot_t(left_ref[...], right_ref[...])
        for b in range(4):
            block = product[b * 64 : b * 64 + 64, b // 2 * 128 : b // 2 * 128 + 128] * w_ref[b % 2]
            high, low = split(block)
            rows = pl.ds(four * 256 + b * 64, 64)
            image_ref[rows, 0:128], image_ref[rows, 128:256] = high, low

    sides(0, 0)

    def pair(gp, _):
        sides(2 * gp + 1, 1)
        image(2 * gp, 0)
        sides(jnp.minimum(2 * gp + 2, 7), 0)
        image(2 * gp + 1, 1)
        return 0

    lax.fori_loop(0, 4, pair, 0)
    lower = lax.broadcasted_iota(jnp.int32, (256, 128), 1) < 64
    for half in range(2):
        image = image_ref[half * 1024 : half * 1024 + 1024]
        turned = dot(image, cols_ref[pl.ds(0, 256)]) + dot(image[:, :128], cols_ref[pl.ds(256, 128)])
        straight, crossed = [], []
        for k in range(2):
            even, odd = turned[k * 512 : k * 512 + 256], turned[k * 512 + 256 : k * 512 + 512]
            straight.append(jnp.where(lower, even, pltpu.roll(odd, 64, 1)))
            crossed.append(jnp.where(lower, pltpu.roll(even, 64, 1), odd))
        total = 0.0
        for part, pieces in enumerate((straight, crossed)):
            high, low = split(jnp.concatenate(pieces, axis=1))
            rows_high, rows_low = joined(rows_ref, 0, part), joined(rows_ref, 1, part)
            total += dot(rows_high, high) + dot(rows_high, low) + dot(rows_low, high)
        for k in range(2):
            for b in range(4):
                sub_ref[pl.ds((half * 2 + k) * 4 + b, SUB, stride=17), :] = total[
                    b * 32 : b * 32 + 32, k * 128 : k * 128 + 128
                ]


def column_transform(grid, wide_ref, twist_ref, last_ref):
    high, low = split(grid)
    wide_high, wide_low = joined(wide_ref, 0), joined(wide_ref, 1)
    wide = dot(high, wide_high) + dot(low, wide_high) + dot(high, wide_low)
    real = wide[:SUB, :TILES] - wide[SUB:, TILES:]
    imag = wide[SUB:, :TILES] + wide[:SUB, TILES:]
    real, imag = cmul(real, imag, twist_ref[0], twist_ref[1])
    high, low = split(jnp.concatenate([real, imag], axis=0))
    return dot(last_ref[0], high) + dot(last_ref[0], low) + dot(last_ref[1], high)


def kernel(
    vis_hbm,
    off_hbm,
    freq_hbm,
    taper_hbm,
    owner_hbm,
    tile_hbm,
    rows_hbm,
    cols_hbm,
    wide_hbm,
    twist_hbm,
    last_hbm,
    out_ref,
    vis_ref,
    off_ref,
    freq_ref,
    taper_ref,
    owner_ref,
    tile_ref,
    rows_ref,
    cols_ref,
    wide_ref,
    twist_ref,
    last_ref,
    w_ref,
    place_ref,
    base_ref,
    far_ref,
    left_a_ref,
    right_a_ref,
    left_b_ref,
    right_b_ref,
    image_ref,
    sub_ref,
    send_ref,
    got_ref,
    places_ref,
    data_ref,
    onehot_ref,
    masked_ref,
    own_ref,
    xsend_ref,
    xgot_ref,
    zsend_ref,
    zgot_ref,
    local_sem,
    psend_sem,
    pgot_sem,
    ssend_sem,
    sgot_sem,
    xsend_sem,
    xgot_sem,
    zsend_sem,
    zgot_sem,
):
    bl, row, col = lax.axis_index("bl"), lax.axis_index("row"), lax.axis_index("col")
    high_z, low_z = bl // 4, bl % 4
    x, y_hi = row // 2, row % 2
    me = y_hi * 32 + low_z * 8 + col

    def member(slot):
        return (high_z * 4 + slot % 32 // 8, x * 2 + slot // 32, slot % 8)

    def along_x(step):
        return (bl, (x + step) % 4 * 2 + y_hi, col)

    def along_z(step):
        return ((high_z + step) % 4 * 4 + low_z, row, col)

    loads = [
        pltpu.make_async_copy(source, target, local_sem.at[k])
        for k, (source, target) in enumerate(
            (
                (off_hbm, off_ref),
                (freq_hbm, freq_ref),
                (taper_hbm, taper_ref),
                (owner_hbm, owner_ref),
                (tile_hbm, tile_ref),
                (vis_hbm, vis_ref),
                (rows_hbm, rows_ref),
                (cols_hbm, cols_ref),
                (twist_hbm, twist_ref),
                (last_hbm, last_ref),
                (wide_hbm, wide_ref),
            )
        )
    ]
    for load in loads:
        load.start()
    barrier = pltpu.get_barrier_semaphore()

    def greet(step, _):
        pl.semaphore_signal(
            barrier, inc=1, device_id=member((me + step) % GROUP), device_id_type=MESH
        )
        return 0

    lax.fori_loop(1, GROUP, greet, 0)
    for step in range(1, 4):
        pl.semaphore_signal(barrier, inc=1, device_id=along_x(step), device_id_type=MESH)
        pl.semaphore_signal(barrier, inc=1, device_id=along_z(step), device_id_type=MESH)
    for load in loads[:5]:
        load.wait()
    places(owner_ref, tile_ref, place_ref)
    phasors(off_ref, freq_ref, base_ref, far_ref)
    weights(taper_ref, w_ref)
    pl.semaphore_wait(barrier, GROUP - 1 + 6)

    def place_copy(step):
        return pltpu.make_async_remote_copy(
            src_ref=place_ref,
            dst_ref=places_ref.at[me],
            send_sem=psend_sem.at[step],
            recv_sem=pgot_sem.at[me],
            device_id=member((me + step) % GROUP),
            device_id_type=MESH,
        )

    def sub_copy(step):
        slot = (me + step) % GROUP
        return pltpu.make_async_remote_copy(
            src_ref=send_ref.at[slot % 32],
            dst_ref=got_ref.at[me],
            send_sem=ssend_sem.at[step],
            recv_sem=sgot_sem.at[me],
            device_id=member(slot),
            device_id_type=MESH,
        )

    def start(copy):
        def body(step, _):
            copy(step).start()
            return 0

        lax.fori_loop(1, GROUP, body, 0)

    def finish_sends(copy):
        def body(step, _):
            copy(step).wait_send()
            return 0

        lax.fori_loop(1, GROUP, body, 0)

    def finish_gets(buffer, sem):
        def body(step, _):
            slot = (me + step) % GROUP
            pltpu.make_async_copy(buffer.at[slot], buffer.at[slot], sem.at[slot]).wait()
            return 0

        lax.fori_loop(1, GROUP, body, 0)

    start(place_copy)
    places_ref[me] = place_ref[...]
    for load in loads[5:8]:
        load.wait()
    side_refs = ((left_a_ref, right_a_ref), (left_b_ref, right_b_ref))
    subgrids(vis_ref, w_ref, rows_ref, cols_ref, base_ref, far_ref, side_refs, image_ref, sub_ref)
    for p in range(SUB):
        send_ref[p] = sub_ref[p * 17 : p * 17 + 16].astype(BF16)
    start(sub_copy)
    got_ref[me] = send_ref[me % 32]

    finish_gets(places_ref, pgot_sem)
    diagonal = (
        lax.broadcasted_iota(jnp.int32, (8, 128), 1) // 16
        == lax.broadcasted_iota(jnp.int32, (8, 128), 0)
    )
    tile_rows = []
    for k in range(16):
        pieces = places_ref[pl.ds(k // 2 * 8, 8), 0, pl.ds(k % 2 * 128, 128)]
        place = jnp.sum(jnp.where(diagonal, pieces, 0), axis=0, keepdims=True)
        tile_rows.append(place // TILES)
        onehot_ref[:, pl.ds(k * 128, 128)] = (
            (lax.broadcasted_iota(jnp.int32, (TILES, 128), 0) == place % TILES)
            .astype(F32)
            .astype(BF16)
        )
    tile_row = jnp.concatenate(tile_rows, axis=1)

    finish_gets(got_ref, sgot_sem)
    for k in range(8):
        turned = got_ref[pl.ds(k * 8, 8)].reshape(128, 128).astype(F32).T.astype(BF16)
        data_ref[:, pl.ds(k * 256, 128)] = turned[:64]
        data_ref[:, pl.ds(k * 256 + 128, 128)] = turned[64:]

    def x_copy(turn, step):
        return pltpu.make_async_remote_copy(
            src_ref=xsend_ref.at[turn, step - 1],
            dst_ref=xgot_ref.at[turn, step - 1],
            send_sem=xsend_sem.at[turn, step - 1],
            recv_sem=xgot_sem.at[turn, step - 1],
            device_id=along_x(step),
            device_id_type=MESH,
        )

    def z_copy(turn):
        return pltpu.make_async_remote_copy(
            src_ref=zsend_ref.at[turn],
            dst_ref=zgot_ref.at[turn],
            send_sem=zsend_sem.at[turn],
            recv_sem=zgot_sem.at[turn],
            device_id=along_z((2, 1, 3)[turn]),
            device_id_type=MESH,
        )

    for turn in range(4):
        td = (high_z + (2, 1, 3, 0)[turn]) % 4
        for step in range(4):
            wanted = ((x + step) % 4 * 2 + y_hi) * 4 + td
            masked_ref[pl.ds(step * 64, 64), :] = jnp.where(
                tile_row == wanted, data_ref[...].astype(F32), 0.0
            ).astype(BF16)
        placed = dot_t(masked_ref[...], onehot_ref[...])
        own_ref[turn] = placed[:64]
        for step in (2, 1, 3):
            xsend_ref[turn, step - 1] = placed[step * 64 : step * 64 + 64].astype(BF16)
            x_copy(turn, step).start()

    for turn in range(4):
        total = own_ref[turn]
        for step in range(1, 4):
            x_copy(turn, step).wait_recv()
            total += xgot_ref[turn, step - 1].astype(F32)
        if turn < 3:
            zsend_ref[turn] = total.astype(BF16)
            z_copy(turn).start()
        else:
            own_ref[turn] = total

    finish_sends(place_copy)
    finish_sends(sub_copy)
    for turn in range(4):
        for step in range(1, 4):
            x_copy(turn, step).wait_send()
    for load in loads[8:]:
        load.wait()
    grid = own_ref[3]
    for turn in range(3):
        z_copy(turn).wait_recv()
        grid += zgot_ref[turn].astype(F32)
    out_ref[...] = column_transform(grid, wide_ref, twist_ref, last_ref)
    for turn in range(3):
        z_copy(turn).wait_send()


def on_device(visibilities, offsets, frequencies, taper_curve, owner_index, tile_index):
    rows, cols, wide, twist, last = (jnp.asarray(table) for table in make_tables())
    operands = (
        visibilities,
        offsets.reshape(64, 64),
        frequencies.reshape(1, 16),
        taper_curve.reshape(1, SUB),
        owner_index.reshape(1, 32),
        tile_index.reshape(1, 32),
        rows,
        cols,
        wide,
        twist,
        last,
    )
    result = pl.pallas_call(
        kernel,
        out_shape=jax.ShapeDtypeStruct((64, TILES), F32),
        in_specs=[pl.BlockSpec(memory_space=pl.ANY)] * len(operands),
        out_specs=pl.BlockSpec(memory_space=pltpu.VMEM),
        scratch_shapes=[pltpu.VMEM(operand.shape, operand.dtype) for operand in operands]
        + [
            pltpu.VMEM((2, 64, 128), F32),
            pltpu.VMEM((1, 256), jnp.int32),
            pltpu.VMEM((2, 8, 520, 128), F32),
            pltpu.VMEM((2, 2, 64, 1024), F32),
            pltpu.VMEM((256, 1024), BF16),
            pltpu.VMEM((256, 1024), BF16),
            pltpu.VMEM((256, 1024), BF16),
            pltpu.VMEM((256, 1024), BF16),
            pltpu.VMEM((2048, 256), BF16),
            pltpu.VMEM((17 * SUB, 128), F32),
            pltpu.VMEM((SUB, 16, 128), BF16),
            pltpu.VMEM((GROUP, 16, 128), BF16),
            pltpu.VMEM((GROUP, 1, 256), jnp.int32),
            pltpu.VMEM((64, 2048), BF16),
            pltpu.VMEM((TILES, 2048), BF16),
            pltpu.VMEM((256, 2048), BF16),
            pltpu.VMEM((4, 64, TILES), F32),
            pltpu.VMEM((4, 3, 64, TILES), BF16),
            pltpu.VMEM((4, 3, 64, TILES), BF16),
            pltpu.VMEM((3, 64, TILES), BF16),
            pltpu.VMEM((3, 64, TILES), BF16),
            pltpu.SemaphoreType.DMA((len(operands),)),
            pltpu.SemaphoreType.DMA((GROUP,)),
            pltpu.SemaphoreType.DMA((GROUP,)),
            pltpu.SemaphoreType.DMA((GROUP,)),
            pltpu.SemaphoreType.DMA((GROUP,)),
            pltpu.SemaphoreType.DMA((4, 3)),
            pltpu.SemaphoreType.DMA((4, 3)),
            pltpu.SemaphoreType.DMA((3,)),
            pltpu.SemaphoreType.DMA((3,)),
        ],
        compiler_params=pltpu.CompilerParams(
            collective_id=0, has_side_effects=True, vmem_limit_bytes=60 * 1024 * 1024
        ),
    )(*operands)
    return result.reshape(1, 1, 2, GC)


def solution(mesh):
    in_specs = (
        P(("bl", "row", "col"), None, None),
        P(("bl", "row", "col"), None, None),
        P(),
        P(),
        P(("bl", "row", "col"), None),
        P(("bl", "row", "col")),
    )
    out_specs = P("row", ("bl", "col"), None, None)
    return jax.shard_map(
        on_device, mesh=mesh, in_specs=in_specs, out_specs=out_specs, check_vma=False
    )
```

time: 83 us -> 68.3 us (0.82)
  local copies, waits for them, and re-layouts: 9.37 us -> 1.67 us
  Pallas kernels: 71.2 us -> 66.5 us
  other arithmetic: 1.74 us -> 0 us
    unnamed x14 -> x0, local copies, waits for them, and re-layouts: 6.86 us -> none
    pallas_call x1, Pallas kernels: 71.2 us -> 66.5 us  [on_device(): pl.pallas_call(kernel, out_shape=jax.ShapeDtypeStruct((64, TILES), F32),...]
    another operation x3 -> x0, local copies, waits for them, and re-layouts: 1.41 us -> none  [the longest x2 0.75 us: on_device(): jnp.tile(frequencies, 64).reshape(1, 1024)]
    mul x1 -> x0, other arithmetic: 1.05 us -> none  [on_device(): weights = taper[:, None] * taper[None, :] * mask]
    reshape x1, local copies, waits for them, and re-layouts: 0.76 us -> 1.67 us  [on_device(): return result.reshape(1, 1, 2, GC)]
where the time goes in v2:
time: 68.3 us; the launch traced here: 68.2 us
  Pallas kernels  66.5 us (97%)
  local copies, waits for them, and re-layouts  1.67 us (2%)
    pallas_call x1, Pallas kernels, on_device(): pl.pallas_call(kernel, out_shape=jax.ShapeDtypeStruct((64, TILES), F32),...  66.5 us
    reshape x1, local copies, waits for them, and re-layouts, on_device(): return result.reshape(1, 1, 2, GC)  1.67 us

profile of v2, /device:TPU:1, one launch (start us, length us, event | category | flops | bytes accessed | tf_op | source)
XLA Modules:
  0.0 68.2 jit_solution(4956648332783754898)
XLA Ops:
  0.0 66.5 %shard_map.109 = f32[64,512]{1,0:T(8,128)} custom-call(bf16[32,2,1024]{2,1,0:T(2,128)(2,1)} %vis_hbm.1, bf16[64,64]{1,0:T(8,128)(2,1)} %bitcast.5, f32[1,16]{1,0:T(1,128)} %bitcast.6, f32[1,32]{1,0:T(1,128)} %bitcast.7, s32[1,32]{1,0:T(1,128)} %bitcast.8, s32[1,32]{1,0:T(1,128)} %bitcast.9, bf16[2,2,2,128,128]{4,3,2,1,0:T(8,128)(2,1)} %constant.10.clone.rows_hbm, ...), custom_call_target="tpu_custom_call" | custom-call | tf_op jit(solution)/shard_map/pallas_call | solution.py:511
  66.5 1.7 %reshape.23 = f32[1,1,2,16384]{3,2,1,0:T(2,128)} reshape(f32[64,512]{1,0:T(8,128)} %shard_map.109) | data formatting | bytes 262144 | tf_op jit(solution)/shard_map/reshape | solution.py:553

commit v3 on v2

v3 whole, which is shorter than its diff:
```python
import math

import jax
import jax.numpy as jnp
import numpy as np
from jax import lax
from jax.experimental import pallas as pl
from jax.experimental.pallas import tpu as pltpu
from jax.sharding import PartitionSpec as P

MESH = pl.DeviceIdType.MESH
SUB = 32
GC = 16384
TILES = GC // SUB
F32 = jnp.float32
BF16 = jnp.bfloat16


def split_np(table):
    high = table.astype(BF16)
    low = (table - high.astype(np.float64)).astype(BF16)
    return np.stack([high, low])


def by_lanes(table):
    rows, lanes = table.shape[-2:]
    pieces = table.reshape(table.shape[:-1] + (lanes // 128, 128))
    return np.ascontiguousarray(np.moveaxis(pieces, -2, -3))


def joined(ref, *index):
    return jnp.concatenate([ref[(*index, k)] for k in range(ref.shape[-3])], axis=1)


def make_tables():
    index = np.arange(SUB)
    angle = 2.0 * np.pi * (index[:, None] * index[None, :] % SUB) / SUB
    cos, sin = np.cos(angle), np.sin(angle)
    order = pixel_order()
    cos_in, sin_in = cos[:, order], sin[:, order]
    rows = np.zeros((2, 4, SUB, 4, 2, SUB))
    for b in range(4):
        rows[0, b, :, b, 0], rows[0, b, :, b, 1] = cos_in, sin_in
        rows[1, b, :, b, 0], rows[1, b, :, b, 1] = sin_in, -cos_in
    rows = split_np(rows.reshape(2, 128, 256))
    cos_in, sin_in = cos[order], sin[order]
    straight = np.stack([[cos_in, -sin_in], [sin_in, cos_in]])
    crossed = np.stack([[-sin_in, -cos_in], [cos_in, -sin_in]])
    cols = np.stack([straight, crossed], axis=1)
    cols = cols.reshape(2, 2, 2, SUB, 8, 4).transpose(0, 3, 1, 4, 2, 5).reshape(64, 128)
    cols = split_np(np.tile(cols, (2, 1)))
    cols = np.concatenate([cols[0], cols[0], cols[1]])
    wide = np.arange(TILES)
    wide_angle = 2.0 * np.pi * (wide[:, None] * wide[None, :] % TILES) / TILES
    wide_table = np.concatenate([np.cos(wide_angle), np.sin(wide_angle)], axis=1)
    twist_angle = 2.0 * np.pi * (index[:, None] * wide[None, :]) / GC
    twist = (np.stack([np.cos(twist_angle), np.sin(twist_angle)]) / 128.0).astype(np.float32)
    last = np.block([[cos, -sin], [sin, cos]])
    return (
        by_lanes(rows),
        cols,
        by_lanes(split_np(wide_table)),
        twist,
        split_np(last),
    )


def dot(a, b):
    return lax.dot_general(a, b, (((1,), (0,)), ((), ())), preferred_element_type=F32)


def dot_t(a, b):
    return lax.dot_general(a, b, (((1,), (1,)), ((), ())), preferred_element_type=F32)


def split(x):
    high = x.astype(BF16)
    return high, (x - high.astype(F32)).astype(BF16)


def cmul(ar, ai, br, bi):
    return ar * br - ai * bi, ar * bi + ai * br


def three(x, rows):
    high = x.astype(BF16).astype(F32)
    middle = (x - high).astype(BF16).astype(F32)
    low = x - high - middle
    place = lax.broadcasted_iota(jnp.int32, (rows, x.shape[1]), 0)
    parts = jnp.where(place == 0, high, jnp.where(place == 1, middle, jnp.where(place == 2, low, 0.0)))
    return parts.astype(BF16)


def matches(shape, left, right):
    row, lane = lax.broadcasted_iota(jnp.int32, shape, 0), lax.broadcasted_iota(jnp.int32, shape, 1)
    return (left(row) == right(lane)).astype(F32).astype(BF16)


def pixel(k):
    slot = k % SUB
    return 16 + jnp.where(slot < 16, slot, jnp.where(slot == 16, -16, 16 - slot))


def weights(taper_ref, w_ref):
    parts = three(taper_ref[...], 16)
    along = dot(parts, matches((SUB, 128), lambda i: i, pixel))
    down = dot_t(matches((64, SUB), pixel, lambda k: k), parts)
    along, down = jnp.sum(along, axis=0, keepdims=True), jnp.sum(down, axis=1, keepdims=True)
    lane = lax.broadcasted_iota(jnp.int32, (64, 128), 1) // 64
    for half in range(2):
        w_ref[half] = jnp.where(lane == half, down * along * (1.0 / 1024.0), 0.0)


def place_order(lane):
    slot = lane % SUB
    return slot // 16 * 16 + slot // 4 % 2 * 8 + slot // 8 % 2 * 4 + slot % 4


def places(owner_ref, tile_ref, place_ref):
    row = lax.broadcasted_iota(jnp.int32, (16, SUB), 0)
    parts = jnp.where(row == 0, owner_ref[...], jnp.where(row == 1, tile_ref[...], 0))
    order = matches((SUB, 128), lambda i: i, place_order)
    both = dot(parts.astype(F32).astype(BF16), order).astype(jnp.int32)
    owner, tile = both[0:1], both[1:2]
    place_ref[...] = (owner // 8 * 4 + tile // 64) * TILES + owner % 8 * 64 + tile % 64


def phasors(off_ref, freq_ref, base_ref, far_ref):
    spread = matches((64, 1024), lambda i: i, lambda k: k // 16)
    repeat = matches((16, 1024), lambda i: i, lambda k: k % 16)
    freq = jnp.sum(dot(three(freq_ref[...], 16), repeat), axis=0, keepdims=True)
    scaled = dot(off_ref[...], spread) * freq
    theta = scaled * (2.0 * math.pi / SUB)
    square = theta * theta
    cos = jnp.full_like(square, -1.0 / math.factorial(14))
    sin = jnp.full_like(square, -1.0 / math.factorial(15))
    for order in range(6, -1, -1):
        sign = 1.0 if order % 2 == 0 else -1.0
        cos = cos * square + sign / math.factorial(2 * order)
        sin = sin * square + sign / math.factorial(2 * order + 1)
    z = [(jnp.ones_like(cos), jnp.zeros_like(cos)), (cos, sin * theta)]
    for p in range(2, 8):
        z.append(cmul(*z[p // 2], *z[p - p // 2]))
    for p in range(8):
        for part in range(2):
            for k in range(8):
                base_ref[part, k, pl.ds(p * 65, 64)] = z[p][part][:, k * 128 : k * 128 + 128]
    z8 = cmul(*z[4], *z[4])
    for e, value in enumerate((z8, cmul(*z8, *z8))):
        for part in range(2):
            far_ref[e, part] = value[part]


def pixel_order():
    slot = np.arange(SUB)
    return 16 + np.where(slot < 16, slot, np.where(slot == 16, -16, 16 - slot))


def block_sides(block, slot, vis_ref, base_ref, far_ref, left_ref, right_ref):
    chunk = 256
    first = lax.broadcasted_iota(jnp.int32, (8, chunk), 0) == 0
    for start in range(0, 1024, chunk):
        lanes = pl.ds(start, chunk)
        for side, target in enumerate((left_ref, right_ref)):
            row = 2 * block + side
            low = [
                jnp.concatenate(
                    [
                        base_ref[part, start // 128 + k, pl.ds(row, 8, stride=65), :]
                        for k in range(chunk // 128)
                    ],
                    axis=1,
                )
                for part in (0, 1)
            ]
            far = [
                [jnp.broadcast_to(far_ref[e, part, pl.ds(row, 1), lanes], (8, chunk)) for part in (0, 1)]
                for e in (0, 1)
            ]
            near = (low, cmul(*low, *far[0]))
            if side == 0:
                vis = vis_ref[block, :, lanes].astype(F32)
                vr, vi = (jnp.broadcast_to(vis[k : k + 1], (8, chunk)) for k in (0, 1))
                products = [(vr * c, vi * s, vr * s, vi * c) for c, s in near]
                plus = [(a - b, d + e) for a, b, d, e in products]
                minus = [(a + b, e - d) for a, b, d, e in products]
                last = cmul(vr, vi, far[1][0], -far[1][1])
            else:
                plus, minus = near, [(c, -s) for c, s in near]
                last = (far[1][0], -far[1][1])
            minus[0] = tuple(jnp.where(first, x, y) for x, y in zip(last, minus[0]))
            for part in range(2):
                for k, pieces in enumerate((plus, minus)):
                    rows = pl.ds(slot * 64 + part * 32 + k * 16, 16)
                    target[rows, lanes] = jnp.concatenate(
                        [piece[part] for piece in pieces], axis=0
                    ).astype(BF16)


def sides(four, which, vis_ref, base_ref, far_ref, side_refs):
    for b in range(4):
        block_sides(four * 4 + b, b, vis_ref, base_ref, far_ref, *side_refs[which])


def images(half, vis_ref, w_ref, base_ref, far_ref, side_refs, image_ref):
    def image(four, which):
        left_ref, right_ref = side_refs[which]
        product = dot_t(left_ref[...], right_ref[...])
        for b in range(4):
            block = product[b * 64 : b * 64 + 64, b // 2 * 128 : b // 2 * 128 + 128] * w_ref[b % 2]
            high, low = split(block)
            rows = pl.ds((four - 4 * half) * 256 + b * 64, 64)
            image_ref[rows, 0:128], image_ref[rows, 128:256] = high, low

    def pair(gp, _):
        sides(2 * gp + 1, 1, vis_ref, base_ref, far_ref, side_refs)
        image(2 * gp, 0)
        sides(jnp.minimum(2 * gp + 2, 7), 0, vis_ref, base_ref, far_ref, side_refs)
        image(2 * gp + 1, 1)
        return 0

    lax.fori_loop(2 * half, 2 * half + 2, pair, 0)


def subgrids(image_ref, rows_ref, cols_ref, out_ref):
    lane = lax.broadcasted_iota(jnp.int32, (256, 128), 1)
    lower = lane < 64
    image = image_ref[...]
    turned = dot(image, cols_ref[pl.ds(0, 256)]) + dot(image[:, :128], cols_ref[pl.ds(256, 128)])
    straight, crossed = [], []
    for k in range(2):
        even, odd = turned[k * 512 : k * 512 + 256], turned[k * 512 + 256 : k * 512 + 512]
        straight.append(jnp.where(lower, even, pltpu.roll(odd, 64, 1)))
        crossed.append(jnp.where(lower, pltpu.roll(even, 64, 1), odd))
    total = 0.0
    for part, pieces in enumerate((straight, crossed)):
        high, low = split(jnp.concatenate(pieces, axis=1))
        rows_high, rows_low = joined(rows_ref, 0, part), joined(rows_ref, 1, part)
        total += dot(rows_high, high) + dot(rows_high, low) + dot(rows_low, high)
    pieces = [
        total[b * 32 : b * 32 + 32, k * 128 : k * 128 + 128] for k in range(2) for b in range(4)
    ]
    group = lane[:32] // 8 % 8
    for bit in (1, 2, 4):
        clear = group & bit == 0
        for t in range(8):
            if t & bit == 0:
                x, y = pieces[t], pieces[t | bit]
                pieces[t] = jnp.where(clear, x, pltpu.roll(y, bit * 8, 1))
                pieces[t | bit] = jnp.where(clear, pltpu.roll(x, 128 - bit * 8, 1), y)
    for h in range(4):
        for l in range(4):
            both = [pieces[h * 2 + y][l * 8 : l * 8 + 8] for y in range(2)]
            out_ref[h * 4 + l] = jnp.concatenate(both, axis=0).astype(BF16)


def column_transform(grid, wide_ref, twist_ref, last_ref):
    high, low = split(grid)
    wide_high, wide_low = joined(wide_ref, 0), joined(wide_ref, 1)
    wide = dot(high, wide_high) + dot(low, wide_high) + dot(high, wide_low)
    real = wide[:SUB, :TILES] - wide[SUB:, TILES:]
    imag = wide[SUB:, :TILES] + wide[:SUB, TILES:]
    real, imag = cmul(real, imag, twist_ref[0], twist_ref[1])
    high, low = split(jnp.concatenate([real, imag], axis=0))
    return dot(last_ref[0], high) + dot(last_ref[0], low) + dot(last_ref[1], high)


def kernel(
    vis_hbm,
    off_hbm,
    freq_hbm,
    taper_hbm,
    owner_hbm,
    tile_hbm,
    rows_hbm,
    cols_hbm,
    wide_hbm,
    twist_hbm,
    last_hbm,
    out_ref,
    vis_ref,
    off_ref,
    freq_ref,
    taper_ref,
    owner_ref,
    tile_ref,
    rows_ref,
    cols_ref,
    wide_ref,
    twist_ref,
    last_ref,
    w_ref,
    place_ref,
    base_ref,
    far_ref,
    left_a_ref,
    right_a_ref,
    left_b_ref,
    right_b_ref,
    image_ref,
    zplace_ref,
    yplace_ref,
    zsend_ref,
    zgot_ref,
    turn_ref,
    ysend_ref,
    ygot_ref,
    onehot_ref,
    masked_ref,
    xsend_ref,
    xgot_ref,
    lsend_ref,
    lgot_ref,
    local_sem,
    zplace_send,
    zplace_recv,
    yplace_send,
    yplace_recv,
    z_send,
    z_recv,
    y_send,
    y_recv,
    x_send,
    x_recv,
    l_send,
    l_recv,
):
    loads = [
        pltpu.make_async_copy(source, target, local_sem.at[k])
        for k, (source, target) in enumerate(
            (
                (off_hbm, off_ref),
                (freq_hbm, freq_ref),
                (taper_hbm, taper_ref),
                (owner_hbm, owner_ref),
                (tile_hbm, tile_ref),
                (vis_hbm, vis_ref),
                (rows_hbm, rows_ref),
                (cols_hbm, cols_ref),
                (twist_hbm, twist_ref),
                (last_hbm, last_ref),
                (wide_hbm, wide_ref),
            )
        )
    ]
    for load in loads:
        load.start()

    bl, row, col = lax.axis_index("bl"), lax.axis_index("row"), lax.axis_index("col")
    high_z, low_z = bl // 4, bl % 4
    x, y_hi = row // 2, row % 2
    me = y_hi * 8 + col

    def along_z(slot):
        return (slot, row, col)

    def along_y(slot):
        return (bl, x * 2 + slot // 8, slot % 8)

    def along_x(step):
        return (bl, (x + step) % 4 * 2 + y_hi, col)

    def final(step):
        return ((high_z + step % 4) % 4 * 4 + low_z, x * 2 + (y_hi + step // 4) % 2, col)

    barrier = pltpu.get_barrier_semaphore()

    def greet(device):
        pl.semaphore_signal(barrier, inc=1, device_id=device, device_id_type=MESH)

    def greet_lines(step, _):
        greet(along_z((bl + step) % 16))
        greet(along_y((me + step) % 16))
        return 0

    lax.fori_loop(1, 16, greet_lines, 0)
    for step in range(1, 4):
        greet(along_x(step))
        greet(final(4 + step))

    for load in loads[:5]:
        load.wait()
    places(owner_ref, tile_ref, place_ref)
    phasors(off_ref, freq_ref, base_ref, far_ref)
    weights(taper_ref, w_ref)
    pl.semaphore_wait(barrier, 36)

    def remote(source, target, send_sem, recv_sem, device):
        return pltpu.make_async_remote_copy(
            src_ref=source,
            dst_ref=target,
            send_sem=send_sem,
            recv_sem=recv_sem,
            device_id=device,
            device_id_type=MESH,
        )

    def zplace_copy(slot):
        return remote(
            place_ref, zplace_ref.at[bl], zplace_send.at[slot], zplace_recv.at[bl], along_z(slot)
        )

    def yplace_copy(slot):
        return remote(
            zplace_ref, yplace_ref.at[me], yplace_send.at[slot], yplace_recv.at[me], along_y(slot)
        )

    def z_copy(half):
        return lambda slot: remote(
            zsend_ref.at[half, slot],
            zgot_ref.at[half, bl],
            z_send.at[half, slot],
            z_recv.at[half, bl],
            along_z(slot),
        )

    def y_copy(half):
        return lambda slot: remote(
            ysend_ref.at[half, slot],
            ygot_ref.at[half, me],
            y_send.at[half, slot],
            y_recv.at[half, me],
            along_y(slot),
        )

    def others(mine, act):
        def body(step, _):
            act((mine + step) % 16)
            return 0

        lax.fori_loop(1, 16, body, 0)

    def arrive(mine, buffer, sem):
        def wait(slot):
            pltpu.make_async_copy(buffer.at[slot], buffer.at[slot], sem.at[slot]).wait()

        others(mine, wait)

    others(bl, lambda slot: zplace_copy(slot).start())
    zplace_ref[bl] = place_ref[...]
    for load in loads[5:8]:
        load.wait()
    side_refs = ((left_a_ref, right_a_ref), (left_b_ref, right_b_ref))
    sides(0, 0, vis_ref, base_ref, far_ref, side_refs)
    for half in range(2):
        images(half, vis_ref, w_ref, base_ref, far_ref, side_refs, image_ref)
        subgrids(image_ref, rows_ref, cols_ref, zsend_ref.at[half])
        others(bl, lambda slot: z_copy(half)(slot).start())
        zgot_ref[half, bl] = zsend_ref[half, bl]
        if half == 0:
            arrive(bl, zplace_ref, zplace_recv)
            others(me, lambda slot: yplace_copy(slot).start())
            yplace_ref[me] = zplace_ref[...]

    def turn(half):
        arrive(bl, zgot_ref.at[half], z_recv.at[half])
        for slot in range(16):
            turn_ref[pl.ds(slot * 17, 16)] = zgot_ref[half, slot].astype(F32)
        for slot in range(16):
            ysend_ref[half, slot] = turn_ref[pl.ds(slot, 16, stride=17)].astype(BF16)
        others(me, lambda slot: y_copy(half)(slot).start())
        ygot_ref[half, me] = ysend_ref[half, me]

    turn(0)
    arrive(me, yplace_ref, yplace_recv)
    place = yplace_ref[...].reshape(256, 128).astype(F32).T[:SUB].astype(jnp.int32)
    wanted = (place // TILES - x * 8 + 32) % 32
    column = place % TILES
    tiles = lax.broadcasted_iota(jnp.int32, (TILES, 256), 0)
    for n in range(SUB):
        onehot_ref[n // 16, :, pl.ds(n % 16 * 256, 256)] = (
            (tiles == column[n : n + 1]).astype(F32).astype(BF16)
        )
    turn(1)

    placed = 0.0
    for half in range(2):
        arrive(me, ygot_ref.at[half], y_recv.at[half])
        data = ygot_ref[half].reshape(256, 128).astype(F32).T
        for j in range(16):
            values = data[j * 8 : j * 8 + 8]
            row_of = wanted[half * 16 + j : half * 16 + j + 1]
            for k in range(16):
                pieces = [jnp.where(row_of == 2 * k + e, values, 0.0) for e in range(2)]
                masked_ref[half, pl.ds(k * 16, 16), pl.ds(j * 256, 256)] = jnp.concatenate(
                    pieces, axis=0
                ).astype(BF16)
        placed += dot_t(masked_ref[half], onehot_ref[half])

    def x_copy(step):
        return remote(
            xsend_ref.at[step - 1],
            xgot_ref.at[step - 1],
            x_send.at[step - 1],
            x_recv.at[step - 1],
            along_x(step),
        )

    for step in (2, 1, 3):
        xsend_ref[step - 1] = placed[step * 64 : step * 64 + 64].astype(BF16)
        x_copy(step).start()
    total = placed[:64]
    for step in (1, 3, 2):
        x_copy(step).wait_recv()
        total += xgot_ref[step - 1].astype(F32)

    mine = high_z * 2 + y_hi

    def l_copy(step):
        target = (y_hi + step // 4) % 2 * 4 + (high_z + step % 4) % 4
        return remote(
            lsend_ref.at[target], lgot_ref.at[mine], l_send.at[step], l_recv.at[mine], final(step)
        )

    for m in range(8):
        piece = total[m * 8 : m * 8 + 8]
        lsend_ref[m] = jnp.concatenate([piece[:, :256], piece[:, 256:]], axis=0).astype(BF16)
    for step in (2, 6, 1, 3, 5, 7, 4):
        l_copy(step).start()
    lgot_ref[mine] = lsend_ref[y_hi * 4 + high_z]

    others(bl, lambda slot: zplace_copy(slot).wait_send())
    others(me, lambda slot: yplace_copy(slot).wait_send())
    for half in range(2):
        others(bl, lambda slot: z_copy(half)(slot).wait_send())
        others(me, lambda slot: y_copy(half)(slot).wait_send())
    for step in range(1, 4):
        x_copy(step).wait_send()
    for load in loads[8:]:
        load.wait()

    for step in range(1, 8):
        source = (high_z + step % 4) % 4 * 2 + (y_hi + step // 4) % 2
        pltpu.make_async_copy(lgot_ref.at[source], lgot_ref.at[source], l_recv.at[source]).wait()
    upper = lax.broadcasted_iota(jnp.int32, (8, TILES), 0) < 4
    real, imag = [], []
    for h in range(4):
        even, odd = (
            jnp.concatenate([piece[:8], piece[8:]], axis=1)
            for piece in (lgot_ref[2 * h].astype(F32), lgot_ref[2 * h + 1].astype(F32))
        )
        real.append(jnp.where(upper, even, pltpu.roll(odd, 4, 0)))
        imag.append(jnp.where(upper, pltpu.roll(even, 4, 0), odd))
    grid = jnp.concatenate(real + imag, axis=0)
    result = column_transform(grid, wide_ref, twist_ref, last_ref)
    for part in range(2):
        for k in range(4):
            out_ref[pl.ds(k * 2 + part, SUB, stride=8), :] = result[
                part * 32 : part * 32 + 32, k * 128 : k * 128 + 128
            ]
    for step in range(1, 8):
        l_copy(step).wait_send()


def on_device(visibilities, offsets, frequencies, taper_curve, owner_index, tile_index):
    rows, cols, wide, twist, last = (jnp.asarray(table) for table in make_tables())
    operands = (
        visibilities,
        offsets.reshape(64, 64),
        frequencies.reshape(1, 16),
        taper_curve.reshape(1, SUB),
        owner_index.reshape(1, 32),
        tile_index.reshape(1, 32),
        rows,
        cols,
        wide,
        twist,
        last,
    )
    result = pl.pallas_call(
        kernel,
        out_shape=jax.ShapeDtypeStruct((256, 128), F32),
        in_specs=[pl.BlockSpec(memory_space=pl.ANY)] * len(operands),
        out_specs=pl.BlockSpec(memory_space=pltpu.VMEM),
        scratch_shapes=[pltpu.VMEM(operand.shape, operand.dtype) for operand in operands]
        + [
            pltpu.VMEM((2, 64, 128), F32),
            pltpu.VMEM((1, 128), jnp.int32),
            pltpu.VMEM((2, 8, 520, 128), F32),
            pltpu.VMEM((2, 2, 64, 1024), F32),
            pltpu.VMEM((256, 1024), BF16),
            pltpu.VMEM((256, 1024), BF16),
            pltpu.VMEM((256, 1024), BF16),
            pltpu.VMEM((256, 1024), BF16),
            pltpu.VMEM((1024, 256), BF16),
            pltpu.VMEM((16, 1, 128), jnp.int32),
            pltpu.VMEM((16, 16, 1, 128), jnp.int32),
            pltpu.VMEM((2, 16, 16, 128), BF16),
            pltpu.VMEM((2, 16, 16, 128), BF16),
            pltpu.VMEM((16 * 17, 128), F32),
            pltpu.VMEM((2, 16, 16, 128), BF16),
            pltpu.VMEM((2, 16, 16, 128), BF16),
            pltpu.VMEM((2, TILES, 4096), BF16),
            pltpu.VMEM((2, 256, 4096), BF16),
            pltpu.VMEM((3, 64, TILES), BF16),
            pltpu.VMEM((3, 64, TILES), BF16),
            pltpu.VMEM((8, 16, 256), BF16),
            pltpu.VMEM((8, 16, 256), BF16),
            pltpu.SemaphoreType.DMA((len(operands),)),
        ]
        + [pltpu.SemaphoreType.DMA((16,))] * 4
        + [pltpu.SemaphoreType.DMA((2, 16))] * 4
        + [pltpu.SemaphoreType.DMA((3,))] * 2
        + [pltpu.SemaphoreType.DMA((8,))] * 2,
        compiler_params=pltpu.CompilerParams(
            collective_id=0, has_side_effects=True, vmem_limit_bytes=60 * 1024 * 1024
        ),
    )(*operands)
    return result.reshape(128, 2, 128).transpose(1, 0, 2).reshape(1, 1, 2, GC)


def solution(mesh):
    in_specs = (
        P(("bl", "row", "col"), None, None),
        P(("bl", "row", "col"), None, None),
        P(),
        P(),
        P(("bl", "row", "col"), None),
        P(("bl", "row", "col")),
    )
    out_specs = P("row", ("bl", "col"), None, None)
    return jax.shard_map(
        on_device, mesh=mesh, in_specs=in_specs, out_specs=out_specs, check_vma=False
    )
```

time: 68.3 us -> 73 us (1.069)
  Pallas kernels: 66.5 us -> 71.2 us
    pallas_call x1, Pallas kernels: 66.5 us -> 71.2 us  [on_device(): pl.pallas_call(kernel, out_shape=jax.ShapeDtypeStruct((256, 128), F32), i...]
    reshape x1 -> x0, local copies, waits for them, and re-layouts: 1.67 us -> none  [on_device(): return result.reshape(1, 1, 2, GC)]
    unnamed x0 -> x1, local copies, waits for them, and re-layouts: none -> 1.57 us
where the time goes in v3:
time: 73 us; the launch traced here: 72.8 us
  Pallas kernels  71.2 us (98%)
  local copies, waits for them, and re-layouts  1.57 us (2%)
    pallas_call x1, Pallas kernels, on_device(): pl.pallas_call(kernel, out_shape=jax.ShapeDtypeStruct((256, 128), F32), i...  71.2 us
    unnamed x1, local copies, waits for them, and re-layouts  1.57 us

profile of v3, /device:TPU:1, one launch (start us, length us, event | category | flops | bytes accessed | tf_op | source)
XLA Modules:
  0.0 72.8 jit_solution(17354532397103859707)
XLA Ops:
  0.0 71.2 %shard_map.109 = f32[256,128]{1,0:T(8,128)} custom-call(bf16[32,2,1024]{2,1,0:T(2,128)(2,1)} %vis_hbm.1, bf16[64,64]{1,0:T(8,128)(2,1)} %bitcast.11, f32[1,16]{1,0:T(1,128)} %bitcast.12, f32[1,32]{1,0:T(1,128)} %bitcast.13, s32[1,32]{1,0:T(1,128)} %bitcast.14, s32[1,32]{1,0:T(1,128)} %bitcast.15, bf16[2,2,2,128,128]{4,3,2,1,0:T(8,128)(2,1)} %constant.10.clone.rows_hbm, ...), custom_call_target="tpu_custom_call" | custom-call | tf_op jit(solution)/shard_map/pallas_call | solution.py:570
  71.2 1.6 %copy.14 = f32[1,1,2,16384]{3,2,1,0:T(2,128)} copy(f32[1,1,2,16384]{3,2,1,0:T(2,128)} %bitcast.10) | data formatting | bytes 262144

commit v4 on v3

--- a/solution.py
+++ b/solution.py
@@ -383,7 +383,6 @@
     places(owner_ref, tile_ref, place_ref)
     phasors(off_ref, freq_ref, base_ref, far_ref)
     weights(taper_ref, w_ref)
-    pl.semaphore_wait(barrier, 36)
 
     def remote(source, target, send_sem, recv_sem, device):
         return pltpu.make_async_remote_copy(
@@ -424,8 +423,8 @@
         )
 
     def others(mine, act):
-        def body(step, _):
-            act((mine + step) % 16)
+        def body(k, _):
+            act((mine + 8 + k // 2 * (1 - k % 2 * 2)) % 16)
             return 0
 
         lax.fori_loop(1, 16, body, 0)
@@ -436,8 +435,6 @@
 
         others(mine, wait)
 
-    others(bl, lambda slot: zplace_copy(slot).start())
-    zplace_ref[bl] = place_ref[...]
     for load in loads[5:8]:
         load.wait()
     side_refs = ((left_a_ref, right_a_ref), (left_b_ref, right_b_ref))
@@ -445,12 +442,15 @@
     for half in range(2):
         images(half, vis_ref, w_ref, base_ref, far_ref, side_refs, image_ref)
         subgrids(image_ref, rows_ref, cols_ref, zsend_ref.at[half])
+        if half == 0:
+            pl.semaphore_wait(barrier, 36)
+            others(bl, lambda slot: zplace_copy(slot).start())
+            zplace_ref[bl] = place_ref[...]
         others(bl, lambda slot: z_copy(half)(slot).start())
         zgot_ref[half, bl] = zsend_ref[half, bl]
-        if half == 0:
-            arrive(bl, zplace_ref, zplace_recv)
-            others(me, lambda slot: yplace_copy(slot).start())
-            yplace_ref[me] = zplace_ref[...]
+    arrive(bl, zplace_ref, zplace_recv)
+    others(me, lambda slot: yplace_copy(slot).start())
+    yplace_ref[me] = zplace_ref[...]
 
     def turn(half):
         arrive(bl, zgot_ref.at[half], z_recv.at[half])
@@ -462,29 +462,38 @@
         ygot_ref[half, me] = ysend_ref[half, me]
 
     turn(0)
+    turn(1)
+
     arrive(me, yplace_ref, yplace_recv)
     place = yplace_ref[...].reshape(256, 128).astype(F32).T[:SUB].astype(jnp.int32)
-    wanted = (place // TILES - x * 8 + 32) % 32
+    wanted = ((place // TILES - x * 8 + 32) % 32).astype(F32).astype(BF16)
     column = place % TILES
-    tiles = lax.broadcasted_iota(jnp.int32, (TILES, 256), 0)
+    columns = [
+        jnp.where(column // 256 == k, column - k * 256, -1).astype(F32).astype(BF16)
+        for k in range(2)
+    ]
+    tiles = lax.broadcasted_iota(jnp.int32, (256, 256), 0).astype(F32).astype(BF16)
+    one, zero = jnp.ones((256, 256), BF16), jnp.zeros((256, 256), BF16)
     for n in range(SUB):
-        onehot_ref[n // 16, :, pl.ds(n % 16 * 256, 256)] = (
-            (tiles == column[n : n + 1]).astype(F32).astype(BF16)
-        )
-    turn(1)
-
+        for k in range(2):
+            onehot_ref[n // 16, pl.ds(k * 256, 256), pl.ds(n % 16 * 256, 256)] = jnp.where(
+                tiles == columns[k][n : n + 1], one, zero
+            )
+
+    step_down = (lax.broadcasted_iota(jnp.int32, (16, 256), 0) // 8).astype(F32).astype(BF16)
     placed = 0.0
     for half in range(2):
         arrive(me, ygot_ref.at[half], y_recv.at[half])
         data = ygot_ref[half].reshape(256, 128).astype(F32).T
         for j in range(16):
             values = data[j * 8 : j * 8 + 8]
+            values = jnp.concatenate([values, values], axis=0).astype(BF16)
             row_of = wanted[half * 16 + j : half * 16 + j + 1]
+            row_of = jnp.broadcast_to(row_of, (16, 256)) - step_down
             for k in range(16):
-                pieces = [jnp.where(row_of == 2 * k + e, values, 0.0) for e in range(2)]
-                masked_ref[half, pl.ds(k * 16, 16), pl.ds(j * 256, 256)] = jnp.concatenate(
-                    pieces, axis=0
-                ).astype(BF16)
+                masked_ref[half, pl.ds(k * 16, 16), pl.ds(j * 256, 256)] = jnp.where(
+                    row_of == jnp.full((16, 256), 2.0 * k, BF16), values, zero[:16]
+                )
         placed += dot_t(masked_ref[half], onehot_ref[half])
 
     def x_copy(step):

time: 73 us -> 65.1 us (0.89)
  Pallas kernels: 71.2 us -> 63.3 us
    pallas_call x1, Pallas kernels: 71.2 us -> 63.3 us  [on_device(): pl.pallas_call(kernel, out_shape=jax.ShapeDtypeStruct((256, 128), F32), i...]
where the time goes in v4:
time: 65.1 us; the launch traced here: 64.9 us
  Pallas kernels  63.3 us (97%)
  local copies, waits for them, and re-layouts  1.57 us (2%)
    pallas_call x1, Pallas kernels, on_device(): pl.pallas_call(kernel, out_shape=jax.ShapeDtypeStruct((256, 128), F32), i...  63.3 us
    unnamed x1, local copies, waits for them, and re-layouts  1.57 us

profile of v4, /device:TPU:1, one launch (start us, length us, event | category | flops | bytes accessed | tf_op | source)
XLA Modules:
  0.0 64.9 jit_solution(12639499972867231234)
XLA Ops:
  0.0 63.3 %shard_map.109 = f32[256,128]{1,0:T(8,128)} custom-call(bf16[32,2,1024]{2,1,0:T(2,128)(2,1)} %vis_hbm.1, bf16[64,64]{1,0:T(8,128)(2,1)} %bitcast.11, f32[1,16]{1,0:T(1,128)} %bitcast.12, f32[1,32]{1,0:T(1,128)} %bitcast.13, s32[1,32]{1,0:T(1,128)} %bitcast.14, s32[1,32]{1,0:T(1,128)} %bitcast.15, bf16[2,2,2,128,128]{4,3,2,1,0:T(8,128)(2,1)} %constant.10.clone.rows_hbm, ...), custom_call_target="tpu_custom_call" | custom-call | tf_op jit(solution)/shard_map/pallas_call | solution.py:579
  63.3 1.6 %copy.14 = f32[1,1,2,16384]{3,2,1,0:T(2,128)} copy(f32[1,1,2,16384]{3,2,1,0:T(2,128)} %bitcast.10) | data formatting | bytes 262144

commit v5 on v4

--- a/solution.py
+++ b/solution.py
@@ -116,13 +116,13 @@
     return slot // 16 * 16 + slot // 4 % 2 * 8 + slot // 8 % 2 * 4 + slot % 4
 
 
-def places(owner_ref, tile_ref, place_ref):
+def places(owner_ref, tile_ref):
     row = lax.broadcasted_iota(jnp.int32, (16, SUB), 0)
     parts = jnp.where(row == 0, owner_ref[...], jnp.where(row == 1, tile_ref[...], 0))
     order = matches((SUB, 128), lambda i: i, place_order)
-    both = dot(parts.astype(F32).astype(BF16), order).astype(jnp.int32)
-    owner, tile = both[0:1], both[1:2]
-    place_ref[...] = (owner // 8 * 4 + tile // 64) * TILES + owner % 8 * 64 + tile % 64
+    both = dot(parts.astype(F32).astype(BF16), order)
+    lane = lax.broadcasted_iota(jnp.int32, (16, 128), 1)
+    return jnp.where(lane < SUB, both[0:1], both[1:2]).astype(BF16)
 
 
 def phasors(off_ref, freq_ref, base_ref, far_ref):
@@ -202,14 +202,14 @@
         block_sides(four * 4 + b, b, vis_ref, base_ref, far_ref, *side_refs[which])
 
 
-def images(half, vis_ref, w_ref, base_ref, far_ref, side_refs, image_ref):
+def images(vis_ref, w_ref, base_ref, far_ref, side_refs, image_ref):
     def image(four, which):
         left_ref, right_ref = side_refs[which]
         product = dot_t(left_ref[...], right_ref[...])
         for b in range(4):
             block = product[b * 64 : b * 64 + 64, b // 2 * 128 : b // 2 * 128 + 128] * w_ref[b % 2]
             high, low = split(block)
-            rows = pl.ds((four - 4 * half) * 256 + b * 64, 64)
+            rows = pl.ds(four * 256 + b * 64, 64)
             image_ref[rows, 0:128], image_ref[rows, 128:256] = high, low
 
     def pair(gp, _):
@@ -219,13 +219,13 @@
         image(2 * gp + 1, 1)
         return 0
 
-    lax.fori_loop(2 * half, 2 * half + 2, pair, 0)
-
-
-def subgrids(image_ref, rows_ref, cols_ref, out_ref):
+    sides(0, 0, vis_ref, base_ref, far_ref, side_refs)
+    lax.fori_loop(0, 4, pair, 0)
+
+
+def subgrids(image, rows_ref, cols_ref, out_ref):
     lane = lax.broadcasted_iota(jnp.int32, (256, 128), 1)
     lower = lane < 64
-    image = image_ref[...]
     turned = dot(image, cols_ref[pl.ds(0, 256)]) + dot(image[:, :128], cols_ref[pl.ds(256, 128)])
     straight, crossed = [], []
     for k in range(2):
@@ -251,7 +251,7 @@
     for h in range(4):
         for l in range(4):
             both = [pieces[h * 2 + y][l * 8 : l * 8 + 8] for y in range(2)]
-            out_ref[h * 4 + l] = jnp.concatenate(both, axis=0).astype(BF16)
+            out_ref[h * 4 + l, 0:16] = jnp.concatenate(both, axis=0).astype(BF16)
 
 
 def column_transform(grid, wide_ref, twist_ref, last_ref):
@@ -290,7 +290,6 @@
     twist_ref,
     last_ref,
     w_ref,
-    place_ref,
     base_ref,
     far_ref,
     left_a_ref,
@@ -298,8 +297,6 @@
     left_b_ref,
     right_b_ref,
     image_ref,
-    zplace_ref,
-    yplace_ref,
     zsend_ref,
     zgot_ref,
     turn_ref,
@@ -312,10 +309,6 @@
     lsend_ref,
     lgot_ref,
     local_sem,
-    zplace_send,
-    zplace_recv,
-    yplace_send,
-    yplace_recv,
     z_send,
     z_recv,
     y_send,
@@ -368,21 +361,27 @@
     def greet(device):
         pl.semaphore_signal(barrier, inc=1, device_id=device, device_id_type=MESH)
 
-    def greet_lines(step, _):
-        greet(along_z((bl + step) % 16))
-        greet(along_y((me + step) % 16))
-        return 0
-
-    lax.fori_loop(1, 16, greet_lines, 0)
-    for step in range(1, 4):
+    def others(mine, act):
+        def body(k, _):
+            act((mine + 8 + k // 2 * (1 - k % 2 * 2)) % 16)
+            return 0
+
+        lax.fori_loop(1, 16, body, 0)
+
+    for step in (2, 1, 3):
+        greet(final(4 + step))
+    others(bl, lambda slot: greet(along_z(slot)))
+    others(me, lambda slot: greet(along_y(slot)))
+    for step in (2, 1, 3):
         greet(along_x(step))
-        greet(final(4 + step))
 
     for load in loads[:5]:
         load.wait()
-    places(owner_ref, tile_ref, place_ref)
     phasors(off_ref, freq_ref, base_ref, far_ref)
     weights(taper_ref, w_ref)
+    place_rows = places(owner_ref, tile_ref)
+    for slot in range(16):
+        zsend_ref[0, slot, 16:32] = place_rows
 
     def remote(source, target, send_sem, recv_sem, device):
         return pltpu.make_async_remote_copy(
@@ -394,80 +393,63 @@
             device_id_type=MESH,
         )
 
-    def zplace_copy(slot):
-        return remote(
-            place_ref, zplace_ref.at[bl], zplace_send.at[slot], zplace_recv.at[bl], along_z(slot)
-        )
-
-    def yplace_copy(slot):
-        return remote(
-            zplace_ref, yplace_ref.at[me], yplace_send.at[slot], yplace_recv.at[me], along_y(slot)
-        )
-
-    def z_copy(half):
-        return lambda slot: remote(
-            zsend_ref.at[half, slot],
-            zgot_ref.at[half, bl],
-            z_send.at[half, slot],
-            z_recv.at[half, bl],
-            along_z(slot),
-        )
-
-    def y_copy(half):
-        return lambda slot: remote(
-            ysend_ref.at[half, slot],
-            ygot_ref.at[half, me],
-            y_send.at[half, slot],
-            y_recv.at[half, me],
-            along_y(slot),
-        )
-
-    def others(mine, act):
-        def body(k, _):
-            act((mine + 8 + k // 2 * (1 - k % 2 * 2)) % 16)
-            return 0
-
-        lax.fori_loop(1, 16, body, 0)
-
-    def arrive(mine, buffer, sem):
-        def wait(slot):
-            pltpu.make_async_copy(buffer.at[slot], buffer.at[slot], sem.at[slot]).wait()
-
-        others(mine, wait)
+    def part(ref, half, slot):
+        return ref.at[half, slot, pl.ds(0, (32, 16)[half])]
+
+    def z_copy(half, slot):
+        source, target = part(zsend_ref, half, slot), part(zgot_ref, half, bl)
+        return remote(source, target, z_send.at[half], z_recv.at[half], along_z(slot))
+
+    def y_copy(half, slot):
+        source, target = part(ysend_ref, half, slot), part(ygot_ref, half, me)
+        return remote(source, target, y_send.at[half], y_recv.at[half], along_y(slot))
+
+    def wait_all(ref, half, sem):
+        arrived = ref.at[half, pl.ds(0, 15), pl.ds(0, (32, 16)[half])]
+        pltpu.make_async_copy(arrived, arrived, sem.at[half]).wait()
 
     for load in loads[5:8]:
         load.wait()
     side_refs = ((left_a_ref, right_a_ref), (left_b_ref, right_b_ref))
-    sides(0, 0, vis_ref, base_ref, far_ref, side_refs)
+    images(vis_ref, w_ref, base_ref, far_ref, side_refs, image_ref)
     for half in range(2):
-        images(half, vis_ref, w_ref, base_ref, far_ref, side_refs, image_ref)
-        subgrids(image_ref, rows_ref, cols_ref, zsend_ref.at[half])
+        image = image_ref[half * 1024 : half * 1024 + 1024]
+        subgrids(image, rows_ref, cols_ref, zsend_ref.at[half])
+    pl.semaphore_wait(barrier, 36)
+    for half in range(2):
+        others(bl, lambda slot: z_copy(half, slot).start())
+        rows = slice(0, (32, 16)[half])
+        zgot_ref[half, bl, rows] = zsend_ref[half, bl, rows]
+
+    row_of_slot = lax.broadcasted_iota(jnp.int32, (16, 128), 0)
+
+    def turn(half):
+        wait_all(zgot_ref, half, z_recv)
+        for slot in range(16):
+            turn_ref[pl.ds(slot * 17, 16)] = zgot_ref[half, slot, 0:16].astype(F32)
+        for slot in range(16):
+            ysend_ref[half, slot, 0:16] = turn_ref[pl.ds(slot, 16, stride=17)].astype(BF16)
         if half == 0:
-            pl.semaphore_wait(barrier, 36)
-            others(bl, lambda slot: zplace_copy(slot).start())
-            zplace_ref[bl] = place_ref[...]
-        others(bl, lambda slot: z_copy(half)(slot).start())
-        zgot_ref[half, bl] = zsend_ref[half, bl]
-    arrive(bl, zplace_ref, zplace_recv)
-    others(me, lambda slot: yplace_copy(slot).start())
-    yplace_ref[me] = zplace_ref[...]
-
-    def turn(half):
-        arrive(bl, zgot_ref.at[half], z_recv.at[half])
-        for slot in range(16):
-            turn_ref[pl.ds(slot * 17, 16)] = zgot_ref[half, slot].astype(F32)
-        for slot in range(16):
-            ysend_ref[half, slot] = turn_ref[pl.ds(slot, 16, stride=17)].astype(BF16)
-        others(me, lambda slot: y_copy(half)(slot).start())
-        ygot_ref[half, me] = ysend_ref[half, me]
+            places_here = jnp.zeros((16, 128), F32)
+            for slot in range(16):
+                places_here = jnp.where(
+                    row_of_slot == slot, zgot_ref[0, slot, 16:32].astype(F32), places_here
+                )
+            for slot in range(16):
+                ysend_ref[0, slot, 16:32] = places_here.astype(BF16)
+        others(me, lambda slot: y_copy(half, slot).start())
+        rows = slice(0, (32, 16)[half])
+        ygot_ref[half, me, rows] = ysend_ref[half, me, rows]
 
     turn(0)
     turn(1)
 
-    arrive(me, yplace_ref, yplace_recv)
-    place = yplace_ref[...].reshape(256, 128).astype(F32).T[:SUB].astype(jnp.int32)
-    wanted = ((place // TILES - x * 8 + 32) % 32).astype(F32).astype(BF16)
-    column = place % TILES
+    wait_all(ygot_ref, 0, y_recv)
+    place = ygot_ref[0, :, 16:32].reshape(256, 128).astype(F32).T.astype(jnp.int32)
+    owner, tile = place[:SUB], place[SUB : 2 * SUB]
+    wanted = (owner // 8 * 4 + tile // 64 - x * 8 + 32) % 32
+    wanted = wanted.astype(F32).astype(BF16)
+    column = owner % 8 * 64 + tile % 64
     columns = [
         jnp.where(column // 256 == k, column - k * 256, -1).astype(F32).astype(BF16)
         for k in range(2)
@@ -483,8 +465,9 @@
     step_down = (lax.broadcasted_iota(jnp.int32, (16, 256), 0) // 8).astype(F32).astype(BF16)
     placed = 0.0
     for half in range(2):
-        arrive(me, ygot_ref.at[half], y_recv.at[half])
-        data = ygot_ref[half].reshape(256, 128).astype(F32).T
+        if half == 1:
+            wait_all(ygot_ref, 1, y_recv)
+        data = ygot_ref[half, :, 0:16].reshape(256, 128).astype(F32).T
         for j in range(16):
             values = data[j * 8 : j * 8 + 8]
             values = jnp.concatenate([values, values], axis=0).astype(BF16)
@@ -518,7 +501,7 @@
     def l_copy(step):
         target = (y_hi + step // 4) % 2 * 4 + (high_z + step % 4) % 4
         return remote(
-            lsend_ref.at[target], lgot_ref.at[mine], l_send.at[step], l_recv.at[mine], final(step)
+            lsend_ref.at[target], lgot_ref.at[mine], l_send, l_recv, final(step)
         )
 
     for m in range(8):
@@ -528,19 +511,16 @@
         l_copy(step).start()
     lgot_ref[mine] = lsend_ref[y_hi * 4 + high_z]
 
-    others(bl, lambda slot: zplace_copy(slot).wait_send())
-    others(me, lambda slot: yplace_copy(slot).wait_send())
     for half in range(2):
-        others(bl, lambda slot: z_copy(half)(slot).wait_send())
-        others(me, lambda slot: y_copy(half)(slot).wait_send())
+        wait_all(zsend_ref, half, z_send)
+        wait_all(ysend_ref, half, y_send)
     for step in range(1, 4):
         x_copy(step).wait_send()
     for load in loads[8:]:
         load.wait()
 
-    for step in range(1, 8):
-        source = (high_z + step % 4) % 4 * 2 + (y_hi + step // 4) % 2
-        pltpu.make_async_copy(lgot_ref.at[source], lgot_ref.at[source], l_recv.at[source]).wait()
+    seven = lgot_ref.at[pl.ds(0, 7)]
+    pltpu.make_async_copy(seven, seven, l_recv).wait()
     upper = lax.broadcasted_iota(jnp.int32, (8, TILES), 0) < 4
     real, imag = [], []
     for h in range(4):
@@ -557,8 +537,7 @@
             out_ref[pl.ds(k * 2 + part, SUB, stride=8), :] = result[
                 part * 32 : part * 32 + 32, k * 128 : k * 128 + 128
             ]
-    for step in range(1, 8):
-        l_copy(step).wait_send()
+    pltpu.make_async_copy(seven, seven, l_send).wait()
 
 
 def on_device(visibilities, offsets, frequencies, taper_curve, owner_index, tile_index):
@@ -584,21 +563,18 @@
         scratch_shapes=[pltpu.VMEM(operand.shape, operand.dtype) for operand in operands]
         + [
             pltpu.VMEM((2, 64, 128), F32),
-            pltpu.VMEM((1, 128), jnp.int32),
             pltpu.VMEM((2, 8, 520, 128), F32),
             pltpu.VMEM((2, 2, 64, 1024), F32),
             pltpu.VMEM((256, 1024), BF16),
             pltpu.VMEM((256, 1024), BF16),
             pltpu.VMEM((256, 1024), BF16),
             pltpu.VMEM((256, 1024), BF16),
-            pltpu.VMEM((1024, 256), BF16),
-            pltpu.VMEM((16, 1, 128), jnp.int32),
-            pltpu.VMEM((16, 16, 1, 128), jnp.int32),
-            pltpu.VMEM((2, 16, 16, 128), BF16),
-            pltpu.VMEM((2, 16, 16, 128), BF16),
+            pltpu.VMEM((2048, 256), BF16),
+            pltpu.VMEM((2, 16, 32, 128), BF16),
+            pltpu.VMEM((2, 16, 32, 128), BF16),
             pltpu.VMEM((16 * 17, 128), F32),
-            pltpu.VMEM((2, 16, 16, 128), BF16),
-            pltpu.VMEM((2, 16, 16, 128), BF16),
+            pltpu.VMEM((2, 16, 32, 128), BF16),
+            pltpu.VMEM((2, 16, 32, 128), BF16),
             pltpu.VMEM((2, TILES, 4096), BF16),
             pltpu.VMEM((2, 256, 4096), BF16),
             pltpu.VMEM((3, 64, TILES), BF16),
@@ -607,10 +583,9 @@
             pltpu.VMEM((8, 16, 256), BF16),
             pltpu.SemaphoreType.DMA((len(operands),)),
         ]
-        + [pltpu.SemaphoreType.DMA((16,))] * 4
-        + [pltpu.SemaphoreType.DMA((2, 16))] * 4
+        + [pltpu.SemaphoreType.DMA((2,))] * 4
         + [pltpu.SemaphoreType.DMA((3,))] * 2
-        + [pltpu.SemaphoreType.DMA((8,))] * 2,
+        + [pltpu.SemaphoreType.DMA] * 2,
         compiler_params=pltpu.CompilerParams(
             collective_id=0, has_side_effects=True, vmem_limit_bytes=60 * 1024 * 1024
         ),

time: 65.1 us -> 63.6 us (0.977)
  Pallas kernels: 63.3 us -> 61.9 us
    pallas_call x1, Pallas kernels: 63.3 us -> 61.9 us  [on_device(): pl.pallas_call(kernel, out_shape=jax.ShapeDtypeStruct((256, 128), F32), i...]
where the time goes in v5:
time: 63.6 us; the launch traced here: 63.5 us
  Pallas kernels  61.9 us (97%)
  local copies, waits for them, and re-layouts  1.57 us (2%)
    pallas_call x1, Pallas kernels, on_device(): pl.pallas_call(kernel, out_shape=jax.ShapeDtypeStruct((256, 128), F32), i...  61.9 us
    unnamed x1, local copies, waits for them, and re-layouts  1.57 us

profile of v5, /device:TPU:1, one launch (start us, length us, event | category | flops | bytes accessed | tf_op | source)
XLA Modules:
  0.0 63.5 jit_solution(12302904745486442979)
XLA Ops:
  0.0 61.9 %shard_map.109 = f32[256,128]{1,0:T(8,128)} custom-call(bf16[32,2,1024]{2,1,0:T(2,128)(2,1)} %vis_hbm.1, bf16[64,64]{1,0:T(8,128)(2,1)} %bitcast.11, f32[1,16]{1,0:T(1,128)} %bitcast.12, f32[1,32]{1,0:T(1,128)} %bitcast.13, s32[1,32]{1,0:T(1,128)} %bitcast.14, s32[1,32]{1,0:T(1,128)} %bitcast.15, bf16[2,2,2,128,128]{4,3,2,1,0:T(8,128)(2,1)} %constant.10.clone.rows_hbm, ...), custom_call_target="tpu_custom_call" | custom-call | tf_op jit(solution)/shard_map/pallas_call | solution.py:558
  61.9 1.6 %copy.14 = f32[1,1,2,16384]{3,2,1,0:T(2,128)} copy(f32[1,1,2,16384]{3,2,1,0:T(2,128)} %bitcast.10) | data formatting | bytes 262144

commit v6 on v5

--- a/solution.py
+++ b/solution.py
@@ -121,8 +121,8 @@
     parts = jnp.where(row == 0, owner_ref[...], jnp.where(row == 1, tile_ref[...], 0))
     order = matches((SUB, 128), lambda i: i, place_order)
     both = dot(parts.astype(F32).astype(BF16), order)
-    lane = lax.broadcasted_iota(jnp.int32, (16, 128), 1)
-    return jnp.where(lane < SUB, both[0:1], both[1:2]).astype(BF16)
+    lane = lax.broadcasted_iota(jnp.int32, (1, 128), 1)
+    return jnp.where(lane < SUB, both[0:1], both[1:2])
 
 
 def phasors(off_ref, freq_ref, base_ref, far_ref):
@@ -251,7 +251,7 @@
     for h in range(4):
         for l in range(4):
             both = [pieces[h * 2 + y][l * 8 : l * 8 + 8] for y in range(2)]
-            out_ref[h * 4 + l, 0:16] = jnp.concatenate(both, axis=0).astype(BF16)
+            out_ref[h * 4 + l] = jnp.concatenate(both, axis=0).astype(BF16)
 
 
 def column_transform(grid, wide_ref, twist_ref, last_ref):
@@ -297,6 +297,10 @@
     left_b_ref,
     right_b_ref,
     image_ref,
+    place_ref,
+    zplace_ref,
+    yplace_send_ref,
+    yplace_ref,
     zsend_ref,
     zgot_ref,
     turn_ref,
@@ -309,6 +313,10 @@
     lsend_ref,
     lgot_ref,
     local_sem,
+    zplace_send,
+    zplace_recv,
+    yplace_send,
+    yplace_recv,
     z_send,
     z_recv,
     y_send,
@@ -379,9 +387,7 @@
         load.wait()
     phasors(off_ref, freq_ref, base_ref, far_ref)
     weights(taper_ref, w_ref)
-    place_rows = places(owner_ref, tile_ref)
-    for slot in range(16):
-        zsend_ref[0, slot, 16:32] = place_rows
+    place_ref[...] = places(owner_ref, tile_ref)
 
     def remote(source, target, send_sem, recv_sem, device):
         return pltpu.make_async_remote_copy(
@@ -393,20 +399,23 @@
             device_id_type=MESH,
         )
 
-    def part(ref, half, slot):
-        return ref.at[half, slot, pl.ds(0, (32, 16)[half])]
+    def zplace_copy(slot):
+        return remote(place_ref, zplace_ref.at[bl], zplace_send, zplace_recv, along_z(slot))
+
+    def yplace_copy(slot):
+        return remote(yplace_send_ref, yplace_ref.at[me], yplace_send, yplace_recv, along_y(slot))
 
     def z_copy(half, slot):
-        source, target = part(zsend_ref, half, slot), part(zgot_ref, half, bl)
+        source, target = zsend_ref.at[half, slot], zgot_ref.at[half, bl]
         return remote(source, target, z_send.at[half], z_recv.at[half], along_z(slot))
 
     def y_copy(half, slot):
-        source, target = part(ysend_ref, half, slot), part(ygot_ref, half, me)
+        source, target = ysend_ref.at[half, slot], ygot_ref.at[half, me]
         return remote(source, target, y_send.at[half], y_recv.at[half], along_y(slot))
 
-    def wait_all(ref, half, sem):
-        arrived = ref.at[half, pl.ds(0, 15), pl.ds(0, (32, 16)[half])]
-        pltpu.make_async_copy(arrived, arrived, sem.at[half]).wait()
+    def wait_all(ref, sem):
+        fifteen = ref.at[pl.ds(0, 15)]
+        pltpu.make_async_copy(fifteen, fifteen, sem).wait()
 
     for load in loads[5:8]:
         load.wait()
@@ -416,38 +425,33 @@
         image = image_ref[half * 1024 : half * 1024 + 1024]
         subgrids(image, rows_ref, cols_ref, zsend_ref.at[half])
     pl.semaphore_wait(barrier, 36)
+    others(bl, lambda slot: zplace_copy(slot).start())
+    zplace_ref[bl] = place_ref[...]
     for half in range(2):
         others(bl, lambda slot: z_copy(half, slot).start())
-        rows = slice(0, (32, 16)[half])
-        zgot_ref[half, bl, rows] = zsend_ref[half, bl, rows]
-
-    row_of_slot = lax.broadcasted_iota(jnp.int32, (16, 128), 0)
+        zgot_ref[half, bl] = zsend_ref[half, bl]
+    wait_all(zplace_ref, zplace_recv)
+    yplace_send_ref[...] = zplace_ref[...].reshape(16, 128).astype(BF16)
+    others(me, lambda slot: yplace_copy(slot).start())
+    yplace_ref[me] = yplace_send_ref[...]
 
     def turn(half):
-        wait_all(zgot_ref, half, z_recv)
+        wait_all(zgot_ref.at[half], z_recv.at[half])
         for slot in range(16):
-            turn_ref[pl.ds(slot * 17, 16)] = zgot_ref[half, slot, 0:16].astype(F32)
+            turn_ref[pl.ds(slot * 17, 16)] = zgot_ref[half, slot].astype(F32)
         for slot in range(16):
-            ysend_ref[half, slot, 0:16] = turn_ref[pl.ds(slot, 16, stride=17)].astype(BF16)
-        if half == 0:
-            places_here = jnp.zeros((16, 128), F32)
-            for slot in range(16):
-                places_here = jnp.where(
-                    row_of_slot == slot, zgot_ref[0, slot, 16:32].astype(F32), places_here
-                )
-            for slot in range(16):
-                ysend_ref[0, slot, 16:32] = places_here.astype(BF16)
+            ysend_ref[half, slot] = turn_ref[pl.ds(slot, 16, stride=17)].astype(BF16)
         others(me, lambda slot: y_copy(half, slot).start())
-        rows = slice(0, (32, 16)[half])
-        ygot_ref[half, me, rows] = ysend_ref[half, me, rows]
+        ygot_ref[half, me] = ysend_ref[half, me]
 
     turn(0)
     turn(1)
 
-    wait_all(ygot_ref, 0, y_recv)
-    place = ygot_ref[0, :, 16:32].reshape(256, 128).astype(F32).T.astype(jnp.int32)
+    wait_all(yplace_ref, yplace_recv)
+    place = yplace_ref[...].reshape(256, 128).astype(F32).T.astype(jnp.int32)
     owner, tile = place[:SUB], place[SUB : 2 * SUB]
-    wanted = (owner // 8 * 4 + tile // 64 - x * 8 + 32) % 32
+    pencil, down = owner // 8, tile // 64
+    wanted = (pencil // 2 - x + 4) % 4 * 8 + (down - high_z + 4) % 4 * 2 + pencil % 2
     wanted = wanted.astype(F32).astype(BF16)
     column = owner % 8 * 64 + tile % 64
     columns = [
@@ -465,9 +469,8 @@
     step_down = (lax.broadcasted_iota(jnp.int32, (16, 256), 0) // 8).astype(F32).astype(BF16)
     placed = 0.0
     for half in range(2):
-        if half == 1:
-            wait_all(ygot_ref, 1, y_recv)
-        data = ygot_ref[half, :, 0:16].reshape(256, 128).astype(F32).T
+        wait_all(ygot_ref.at[half], y_recv.at[half])
+        data = ygot_ref[half].reshape(256, 128).astype(F32).T
         for j in range(16):
             values = data[j * 8 : j * 8 + 8]
             values = jnp.concatenate([values, values], axis=0).astype(BF16)
@@ -479,43 +482,49 @@
                 )
         placed += dot_t(masked_ref[half], onehot_ref[half])
 
-    def x_copy(step):
+    def x_copy(turns, step):
         return remote(
-            xsend_ref.at[step - 1],
-            xgot_ref.at[step - 1],
-            x_send.at[step - 1],
-            x_recv.at[step - 1],
+            xsend_ref.at[turns, step - 1],
+            xgot_ref.at[turns, step - 1],
+            x_send.at[turns, step - 1],
+            x_recv.at[turns, step - 1],
             along_x(step),
         )
 
-    for step in (2, 1, 3):
-        xsend_ref[step - 1] = placed[step * 64 : step * 64 + 64].astype(BF16)
-        x_copy(step).start()
-    total = placed[:64]
-    for step in (1, 3, 2):
-        x_copy(step).wait_recv()
-        total += xgot_ref[step - 1].astype(F32)
-
     mine = high_z * 2 + y_hi
 
     def l_copy(step):
-        target = (y_hi + step // 4) % 2 * 4 + (high_z + step % 4) % 4
-        return remote(
-            lsend_ref.at[target], lgot_ref.at[mine], l_send, l_recv, final(step)
-        )
-
-    for m in range(8):
-        piece = total[m * 8 : m * 8 + 8]
-        lsend_ref[m] = jnp.concatenate([piece[:, :256], piece[:, 256:]], axis=0).astype(BF16)
-    for step in (2, 6, 1, 3, 5, 7, 4):
-        l_copy(step).start()
-    lgot_ref[mine] = lsend_ref[y_hi * 4 + high_z]
-
+        source = lsend_ref.at[step % 4, (y_hi + step // 4) % 2]
+        return remote(source, lgot_ref.at[mine], l_send, l_recv, final(step))
+
+    for turns in (2, 1, 3, 0):
+        for step in (2, 1, 3):
+            rows = slice(step * 64 + turns * 16, step * 64 + turns * 16 + 16)
+            xsend_ref[turns, step - 1] = placed[rows].astype(BF16)
+            x_copy(turns, step).start()
+    for turns in (2, 1, 3, 0):
+        total = placed[turns * 16 : turns * 16 + 16]
+        for step in (1, 3, 2):
+            x_copy(turns, step).wait_recv()
+            total += xgot_ref[turns, step - 1].astype(F32)
+        for y in range(2):
+            piece = total[y * 8 : y * 8 + 8]
+            lsend_ref[turns, y] = jnp.concatenate([piece[:, :256], piece[:, 256:]], axis=0).astype(
+                BF16
+            )
+        for step in (turns + 4, turns):
+            if step > 0:
+                l_copy(step).start()
+    lgot_ref[mine] = lsend_ref[0, y_hi]
+
+    wait_all(zplace_ref, zplace_send)
+    wait_all(yplace_ref, yplace_send)
     for half in range(2):
-        wait_all(zsend_ref, half, z_send)
-        wait_all(ysend_ref, half, y_send)
-    for step in range(1, 4):
-        x_copy(step).wait_send()
+        wait_all(zsend_ref.at[half], z_send.at[half])
+        wait_all(ysend_ref.at[half], y_send.at[half])
+    for turns in range(4):
+        for step in range(1, 4):
+            x_copy(turns, step).wait_send()
     for load in loads[8:]:
         load.wait()
 
@@ -570,21 +579,26 @@
             pltpu.VMEM((256, 1024), BF16),
             pltpu.VMEM((256, 1024), BF16),
             pltpu.VMEM((2048, 256), BF16),
-            pltpu.VMEM((2, 16, 32, 128), BF16),
-            pltpu.VMEM((2, 16, 32, 128), BF16),
+            pltpu.VMEM((1, 128), F32),
+            pltpu.VMEM((16, 1, 128), F32),
+            pltpu.VMEM((16, 128), BF16),
+            pltpu.VMEM((16, 16, 128), BF16),
+            pltpu.VMEM((2, 16, 16, 128), BF16),
+            pltpu.VMEM((2, 16, 16, 128), BF16),
             pltpu.VMEM((16 * 17, 128), F32),
-            pltpu.VMEM((2, 16, 32, 128), BF16),
-            pltpu.VMEM((2, 16, 32, 128), BF16),
+            pltpu.VMEM((2, 16, 16, 128), BF16),
+            pltpu.VMEM((2, 16, 16, 128), BF16),
             pltpu.VMEM((2, TILES, 4096), BF16),
             pltpu.VMEM((2, 256, 4096), BF16),
-            pltpu.VMEM((3, 64, TILES), BF16),
-            pltpu.VMEM((3, 64, TILES), BF16),
-            pltpu.VMEM((8, 16, 256), BF16),
+            pltpu.VMEM((4, 3, 16, TILES), BF16),
+            pltpu.VMEM((4, 3, 16, TILES), BF16),
+            pltpu.VMEM((4, 2, 16, 256), BF16),
             pltpu.VMEM((8, 16, 256), BF16),
             pltpu.SemaphoreType.DMA((len(operands),)),
         ]
+        + [pltpu.SemaphoreType.DMA] * 4
         + [pltpu.SemaphoreType.DMA((2,))] * 4
-        + [pltpu.SemaphoreType.DMA((3,))] * 2
+        + [pltpu.SemaphoreType.DMA((4, 3))] * 2
         + [pltpu.SemaphoreType.DMA] * 2,
         compiler_params=pltpu.CompilerParams(
             collective_id=0, has_side_effects=True, vmem_limit_bytes=60 * 1024 * 1024

time: 63.6 us -> 59.5 us (0.936)
  Pallas kernels: 61.9 us -> 57.5 us
    pallas_call x1, Pallas kernels: 61.9 us -> 57.5 us  [on_device(): pl.pallas_call(kernel, out_shape=jax.ShapeDtypeStruct((256, 128), F32), i...]
where the time goes in v6:
time: 59.5 us; the launch traced here: 59.1 us
  Pallas kernels  57.5 us (97%)
  local copies, waits for them, and re-layouts  1.57 us (3%)
    pallas_call x1, Pallas kernels, on_device(): pl.pallas_call(kernel, out_shape=jax.ShapeDtypeStruct((256, 128), F32), i...  57.5 us
    unnamed x1, local copies, waits for them, and re-layouts  1.57 us

profile of v6, /device:TPU:1, one launch (start us, length us, event | category | flops | bytes accessed | tf_op | source)
XLA Modules:
  0.0 59.1 jit_solution(6434818426416663350)
XLA Ops:
  0.0 57.5 %shard_map.109 = f32[256,128]{1,0:T(8,128)} custom-call(bf16[32,2,1024]{2,1,0:T(2,128)(2,1)} %vis_hbm.1, bf16[64,64]{1,0:T(8,128)(2,1)} %bitcast.11, f32[1,16]{1,0:T(1,128)} %bitcast.12, f32[1,32]{1,0:T(1,128)} %bitcast.13, s32[1,32]{1,0:T(1,128)} %bitcast.14, s32[1,32]{1,0:T(1,128)} %bitcast.15, bf16[2,2,2,128,128]{4,3,2,1,0:T(8,128)(2,1)} %constant.10.clone.rows_hbm, ...), custom_call_target="tpu_custom_call" | custom-call | tf_op jit(solution)/shard_map/pallas_call | solution.py:567
  57.6 1.6 %copy.14 = f32[1,1,2,16384]{3,2,1,0:T(2,128)} copy(f32[1,1,2,16384]{3,2,1,0:T(2,128)} %bitcast.10) | data formatting | bytes 262144

commit v7 on v6

--- a/solution.py
+++ b/solution.py
@@ -255,9 +255,7 @@
 
 
 def column_transform(grid, wide_ref, twist_ref, last_ref):
-    high, low = split(grid)
-    wide_high, wide_low = joined(wide_ref, 0), joined(wide_ref, 1)
-    wide = dot(high, wide_high) + dot(low, wide_high) + dot(high, wide_low)
+    wide = dot(grid, joined(wide_ref, 0)) + dot(grid, joined(wide_ref, 1))
     real = wide[:SUB, :TILES] - wide[SUB:, TILES:]
     imag = wide[SUB:, :TILES] + wide[:SUB, TILES:]
     real, imag = cmul(real, imag, twist_ref[0], twist_ref[1])
@@ -376,8 +374,6 @@
 
         lax.fori_loop(1, 16, body, 0)
 
-    for step in (2, 1, 3):
-        greet(final(4 + step))
     others(bl, lambda slot: greet(along_z(slot)))
     others(me, lambda slot: greet(along_y(slot)))
     for step in (2, 1, 3):
@@ -424,7 +420,7 @@
     for half in range(2):
         image = image_ref[half * 1024 : half * 1024 + 1024]
         subgrids(image, rows_ref, cols_ref, zsend_ref.at[half])
-    pl.semaphore_wait(barrier, 36)
+    pl.semaphore_wait(barrier, 33)
     others(bl, lambda slot: zplace_copy(slot).start())
     zplace_ref[bl] = place_ref[...]
     for half in range(2):
@@ -539,7 +535,7 @@
         )
         real.append(jnp.where(upper, even, pltpu.roll(odd, 4, 0)))
         imag.append(jnp.where(upper, pltpu.roll(even, 4, 0), odd))
-    grid = jnp.concatenate(real + imag, axis=0)
+    grid = jnp.concatenate(real + imag, axis=0).astype(BF16)
     result = column_transform(grid, wide_ref, twist_ref, last_ref)
     for part in range(2):
         for k in range(4):
@@ -566,7 +562,7 @@
     )
     result = pl.pallas_call(
         kernel,
-        out_shape=jax.ShapeDtypeStruct((256, 128), F32),
+        out_shape=pltpu.VMEM((256, 128), F32),
         in_specs=[pl.BlockSpec(memory_space=pl.ANY)] * len(operands),
         out_specs=pl.BlockSpec(memory_space=pltpu.VMEM),
         scratch_shapes=[pltpu.VMEM(operand.shape, operand.dtype) for operand in operands]

time: 59.5 us -> 55.2 us (0.928)
  Pallas kernels: 57.5 us -> 54.2 us
  local copies, waits for them, and re-layouts: 1.57 us -> 0.66 us
    pallas_call x1, Pallas kernels: 57.5 us -> 54.2 us  [on_device(): pl.pallas_call(kernel, out_shape=pltpu.VMEM((256, 128), F32), in_specs=[p...]
    unnamed x1, local copies, waits for them, and re-layouts: 1.57 us -> 0.66 us
where the time goes in v7:
time: 55.2 us; the launch traced here: 54.9 us
  Pallas kernels  54.2 us (98%)
  local copies, waits for them, and re-layouts  0.66 us (1%)
    pallas_call x1, Pallas kernels, on_device(): pl.pallas_call(kernel, out_shape=pltpu.VMEM((256, 128), F32), in_specs=[p...  54.2 us

profile of v7, /device:TPU:1, one launch (start us, length us, event | category | flops | bytes accessed | tf_op | source)
XLA Modules:
  0.0 54.9 jit_solution(8335557297226873498)
XLA Ops:
  0.0 54.2 %shard_map.109 = f32[256,128]{1,0:T(8,128)S(1)} custom-call(bf16[32,2,1024]{2,1,0:T(2,128)(2,1)} %vis_hbm.1, bf16[64,64]{1,0:T(8,128)(2,1)} %bitcast.11, f32[1,16]{1,0:T(1,128)} %bitcast.12, f32[1,32]{1,0:T(1,128)} %bitcast.13, s32[1,32]{1,0:T(1,128)} %bitcast.14, s32[1,32]{1,0:T(1,128)} %bitcast.15, bf16[2,2,2,128,128]{4,3,2,1,0:T(8,128)(2,1)} %constant.10.clone.rows_hbm, ...), custom_call_target="tpu_custom_call" | custom-call | tf_op jit(solution)/shard_map/pallas_call | solution.py:563
  54.2 0.7 %copy.14 = f32[1,1,2,16384]{3,2,1,0:T(2,128)} copy(f32[1,1,2,16384]{3,2,1,0:T(2,128)S(1)} %bitcast.10) | data formatting | bytes 262144

commit v8 on v7

--- a/solution.py
+++ b/solution.py
@@ -374,6 +374,8 @@
 
         lax.fori_loop(1, 16, body, 0)
 
+    for step in (2, 1, 3):
+        greet(final(4 + step))
     others(bl, lambda slot: greet(along_z(slot)))
     others(me, lambda slot: greet(along_y(slot)))
     for step in (2, 1, 3):
@@ -420,7 +422,7 @@
     for half in range(2):
         image = image_ref[half * 1024 : half * 1024 + 1024]
         subgrids(image, rows_ref, cols_ref, zsend_ref.at[half])
-    pl.semaphore_wait(barrier, 33)
+    pl.semaphore_wait(barrier, 36)
     others(bl, lambda slot: zplace_copy(slot).start())
     zplace_ref[bl] = place_ref[...]
     for half in range(2):
@@ -568,7 +570,7 @@
         scratch_shapes=[pltpu.VMEM(operand.shape, operand.dtype) for operand in operands]
         + [
             pltpu.VMEM((2, 64, 128), F32),
-            pltpu.VMEM((2, 8, 520, 128), F32),
+            pltpu.VMEM((2, 8, 584, 128), F32),
             pltpu.VMEM((2, 2, 64, 1024), F32),
             pltpu.VMEM((256, 1024), BF16),
             pltpu.VMEM((256, 1024), BF16),

time: 55.2 us -> 57.7 us (1.045)
  Pallas kernels: 54.2 us -> 56.7 us
    pallas_call x1, Pallas kernels: 54.2 us -> 56.7 us  [on_device(): pl.pallas_call(kernel, out_shape=pltpu.VMEM((256, 128), F32), in_specs=[p...]
where the time goes in v8:
time: 57.7 us; the launch traced here: 57.4 us
  Pallas kernels  56.7 us (98%)
  local copies, waits for them, and re-layouts  0.66 us (1%)
    pallas_call x1, Pallas kernels, on_device(): pl.pallas_call(kernel, out_shape=pltpu.VMEM((256, 128), F32), in_specs=[p...  56.7 us

profile of v8, /device:TPU:1, one launch (start us, length us, event | category | flops | bytes accessed | tf_op | source)
XLA Modules:
  0.0 57.4 jit_solution(3336484085460181430)
XLA Ops:
  0.0 56.7 %shard_map.109 = f32[256,128]{1,0:T(8,128)S(1)} custom-call(bf16[32,2,1024]{2,1,0:T(2,128)(2,1)} %vis_hbm.1, bf16[64,64]{1,0:T(8,128)(2,1)} %bitcast.11, f32[1,16]{1,0:T(1,128)} %bitcast.12, f32[1,32]{1,0:T(1,128)} %bitcast.13, s32[1,32]{1,0:T(1,128)} %bitcast.14, s32[1,32]{1,0:T(1,128)} %bitcast.15, bf16[2,2,2,128,128]{4,3,2,1,0:T(8,128)(2,1)} %constant.10.clone.rows_hbm, ...), custom_call_target="tpu_custom_call" | custom-call | tf_op jit(solution)/shard_map/pallas_call | solution.py:565
  56.7 0.7 %copy.14 = f32[1,1,2,16384]{3,2,1,0:T(2,128)} copy(f32[1,1,2,16384]{3,2,1,0:T(2,128)S(1)} %bitcast.10) | data formatting | bytes 262144
